TPU v7x, 256 devices: a whole 4x4x8 slice. The times are simulated.
256 devices in a mesh: dp: 32 (over z_hi, x, core), rep: 8 (over z_lo, y).
Axes of the slice: x: 4, y: 4, z: 8 (z_hi: 4, z_lo: 2; z = z_hi * 2 + z_lo), core: 2. Of those that a mesh axis runs over, the one named last changes fastest.
Arguments:
- images: bfloat16 [1536, 14, 14, 256], P(('dp', 'rep')), may hold values from -6 to 6
- labels: int32 [1536], P(('dp', 'rep')), may hold values from 0 to 2047
- conv_one: bfloat16 [3, 3, 256, 256], replicated, may hold values from -0.125 to 0.125
- conv_two: bfloat16 [3, 3, 256, 256], replicated, may hold values from -0.125 to 0.125
- prelu_slope: float32 [256], replicated, may hold values from 0.05 to 0.5
- spatial: float32 [196, 256], replicated, may hold values from -0.4375 to 0.4375
- head_weight: bfloat16 [256, 512], replicated, may hold values from -0.375 to 0.375
- class_queue: bfloat16 [2048, 512], replicated, may hold values from -6 to 6
- candidates: bfloat16 [16384, 512], P(('dp', 'rep')), may hold values from -6 to 6
- generator: int32 [32], replicated, may hold values from 0 to 31, each once
- offset: int32 [1], replicated, may hold values from 0 to 2047
Outputs:
- image_loss: float32 [1536], P(('dp', 'rep'))
- fresh_queue: bfloat16 [2048, 512], replicated
- update: float32 [1310720], P(('dp', 'rep'))
Inputs may be any that keep to these rules, and one draw needn't show every extreme that they name: `generator`: each group index appears exactly once.
All inputs are finite; a program needn't handle non-finite values.
Results may differ from a plain program's by a relative error of at most 0.0054.
Values may be sent and summed in bfloat16 or wider, within the bound.
A program may use at most 128 MiB of HBM per device.

v0:
```python
import jax
import jax.numpy as jnp
from jax import lax
from jax.sharding import PartitionSpec as P


def spread(value, axis, root):
    mine = lax.axis_index(axis) == root
    return lax.psum(jnp.where(mine, value, jnp.zeros_like(value)), axis)


def patches_of(field):
    side_len = field.shape[1]
    padded = jnp.pad(field, ((0, 0), (1, 1), (1, 1), (0, 0)))
    shifted = [
        padded[:, row_shift : row_shift + side_len, col_shift : col_shift + side_len, :]
        for row_shift in range(3)
        for col_shift in range(3)
    ]
    return jnp.concatenate(shifted, axis=3)


def fold_back(grad_patch, channels):
    image_count, side_len = (grad_patch.shape[0], grad_patch.shape[1])
    accum = jnp.zeros((image_count, side_len + 2, side_len + 2, channels), jnp.float32)
    for tap_index in range(9):
        row_shift, col_shift = (tap_index // 3, tap_index % 3)
        tap_block = grad_patch[..., tap_index * channels : (tap_index + 1) * channels]
        accum = accum + jnp.pad(
            tap_block, ((0, 0), (row_shift, 2 - row_shift), (col_shift, 2 - col_shift), (0, 0))
        )
    return accum[:, 1:-1, 1:-1, :]


def refresh(class_queue, class_panel, start_slot):
    rolled = jnp.roll(class_queue, -start_slot, axis=0)
    rolled = jnp.concatenate([class_panel, rolled[class_panel.shape[0] :]], axis=0)
    return jnp.roll(rolled, start_slot, axis=0)


def unit_rows(fresh_queue):
    rows_f = fresh_queue.astype(jnp.float32)
    return rows_f * lax.rsqrt(jnp.sum(rows_f * rows_f, axis=1, keepdims=True) + 1e-06)


def local_step(images, labels, conv_one, conv_two, prelu_slope, spatial, head_weight, unit_queue):
    image_count, side_len, channels = (images.shape[0], images.shape[1], images.shape[3])
    cell_count = image_count * side_len * side_len
    highest = lax.Precision.HIGHEST
    w_one = conv_one.reshape(9 * channels, channels)
    w_two = conv_two.reshape(9 * channels, channels)
    patch_one = patches_of(images).reshape(cell_count, 9 * channels)
    pre_act = jnp.dot(patch_one, w_one, preferred_element_type=jnp.float32)
    hidden = jnp.where(pre_act > 0, pre_act, prelu_slope[None, :] * pre_act).astype(jnp.bfloat16)
    patch_two = patches_of(hidden.reshape(image_count, side_len, side_len, channels)).reshape(
        cell_count, 9 * channels
    )
    block_out = images.reshape(cell_count, channels).astype(jnp.float32) + jnp.dot(
        patch_two, w_two, preferred_element_type=jnp.float32
    )
    pooled = jnp.sum(
        block_out.reshape(image_count, side_len * side_len, channels) * spatial[None], axis=1
    )
    head_f = head_weight.astype(jnp.float32)
    embed = jnp.dot(pooled, head_f, precision=highest)
    inv_len = lax.rsqrt(jnp.sum(embed * embed, axis=1, keepdims=True) + 1e-06)
    unit_embed = embed * inv_len
    slots = unit_queue.shape[0]
    onehot = (labels[:, None] == jnp.arange(slots, dtype=jnp.int32)[None, :]).astype(jnp.float32)
    cosine = jnp.dot(unit_embed, unit_queue.T, precision=highest)
    logits = 64.0 * (cosine - 0.4 * onehot)
    exps = jnp.exp(logits)
    exp_total = jnp.sum(exps, axis=1, keepdims=True)
    image_loss = jnp.log(exp_total[:, 0]) - jnp.sum(logits * onehot, axis=1)
    d_logits = exps / exp_total - onehot
    d_unit = 64.0 * jnp.dot(d_logits, unit_queue, precision=highest)
    d_embed = (d_unit - unit_embed * jnp.sum(d_unit * unit_embed, axis=1, keepdims=True)) * inv_len
    grad_head = jnp.dot(pooled.T, d_embed, precision=highest)
    d_pooled = jnp.dot(d_embed, head_f.T, precision=highest)
    d_block = (
        (d_pooled[:, None, :] * spatial[None]).astype(jnp.bfloat16).reshape(cell_count, channels)
    )
    grad_two = jnp.dot(patch_two.T, d_block, preferred_element_type=jnp.float32)
    grad_patch = jnp.dot(d_block, w_two.T, preferred_element_type=jnp.float32).reshape(
        image_count, side_len, side_len, 9 * channels
    )
    d_hidden = fold_back(grad_patch, channels).reshape(cell_count, channels)
    d_pre = (d_hidden * jnp.where(pre_act > 0, 1.0, prelu_slope[None, :])).astype(jnp.bfloat16)
    grad_one = jnp.dot(patch_one.T, d_pre, preferred_element_type=jnp.float32)
    grad_flat = jnp.concatenate([grad_one.reshape(-1), grad_two.reshape(-1), grad_head.reshape(-1)])
    return (image_loss, grad_flat)


def normalize_update(summed, conv_len):
    segments = [summed[:conv_len], summed[conv_len : 2 * conv_len], summed[2 * conv_len :]]
    scaled = [
        segment
        * jnp.sqrt(jnp.float32(segment.shape[0]))
        * lax.rsqrt(jnp.sum(segment * segment) + 1e-06)
        for segment in segments
    ]
    return jnp.concatenate(scaled)


def shards(
    images,
    labels,
    conv_one,
    conv_two,
    prelu_slope,
    spatial,
    head_weight,
    class_queue,
    candidates,
    generator,
    offset,
):
    source_group = generator[0]
    group_panel = lax.all_gather(candidates, "rep", axis=0, tiled=True)
    class_panel = spread(group_panel, "dp", source_group)
    fresh_queue = refresh(class_queue, class_panel, offset[0])
    unit_queue = unit_rows(fresh_queue)
    image_loss, grad_flat = local_step(
        images, labels, conv_one, conv_two, prelu_slope, spatial, head_weight, unit_queue
    )
    conv_len = conv_one.size
    devices_all = lax.axis_size(("dp", "rep"))
    share_len = grad_flat.shape[0] // devices_all
    start_pos = lax.axis_index(("dp", "rep")) * share_len
    summed = lax.psum(grad_flat, ("dp", "rep"))
    update = lax.dynamic_slice_in_dim(normalize_update(summed, conv_len), start_pos, share_len, 0)
    return (image_loss, fresh_queue, update)


def solution(mesh):
    in_specs = (
        P(("dp", "rep"), None, None, None),
        P(("dp", "rep")),
        P(),
        P(),
        P(),
        P(),
        P(),
        P(),
        P(("dp", "rep"), None),
        P(),
        P(),
    )
    out_specs = (P(("dp", "rep")), P(), P(("dp", "rep")))
    return jax.shard_map(shards, mesh=mesh, in_specs=in_specs, out_specs=out_specs, check_vma=False)
```

profile of v0, /device:TPU:1, one launch (start us, length us, event | category | flops | bytes accessed | tf_op | source)
XLA Modules:
  0.0 673.8 jit_solution(5638598611543222799)
XLA Ops:
  7.2 25.1 %all_gather.3 = bf16[512,512]{1,0:T(8,128)(2,1)S(1)} all-gather(bf16[64,512]{1,0:T(8,128)(2,1)} %param.21), channel_id=1, replica_groups=mesh['dp'=32,'rep'=8] {'rep'}, dimensions={0}, use_global_device_ids=true | all-gather | bytes 589824 | tf_op jit(solution)/shard_map/all_gather | solution.py:119
  33.9 1.2 reshape.86
  35.1 1.1 slice_dynamic-update-slice_fusion.7
  36.2 1.0 slice_dynamic-update-slice_fusion.6
  37.2 1.1 slice_dynamic-update-slice_fusion.5
  38.3 1.2 slice_dynamic-update-slice_fusion.4
  39.5 1.0 constant_dynamic-update-slice_fusion
  40.5 1.1 slice_dynamic-update-slice_fusion.3
  41.6 1.1 slice_dynamic-update-slice_fusion.2
  42.8 1.0 slice_dynamic-update-slice_fusion.1
  43.7 1.1 slice_dynamic-update-slice_fusion
  44.8 9.3 %reshape.77 = bf16[1176,2304]{1,0:T(8,128)(2,1)} reshape(bf16[6,14,14,2304]{3,2,1,0:T(8,128)(2,1)} %slice_dynamic-update-slice_fusion) | data formatting | bytes 10838016 | tf_op jit(solution)/shard_map/reshape | solution.py:52
  54.1 5.2 fusion.13
  60.2 1.0 reshape.79
  61.2 5.2 pad_slice_fusion
  66.4 2.1 concatenate.43
  68.5 2.0 concatenate.37
  70.5 2.0 concatenate.38
  72.6 2.1 concatenate.39
  74.6 2.1 concatenate.40
  76.7 1.0 concatenate.41
  77.9 1.0 concatenate.36
  78.9 1.2 constant_dynamic-update-slice_fusion.9
  80.1 1.2 constant_dynamic-update-slice_fusion.8
  82.7 2.3 copy-done.20
  85.0 2.7 convolution_add_fusion
  87.7 1.5 reshape.81
  91.0 2.9 fusion.10
  93.9 232.6 %all-reduce.14.cloned.1.call-done = bf16[512,512]{1,0:T(8,128)(2,1)} async-done(((bf16[512,512]{1,0:T(8,128)(2,1)}), bf16[512,512]{1,0:T(8,128)(2,1)}) %all-reduce.14.cloned.1.call-update) | async-done | bytes 524304 | tf_op jit(solution)/shard_map/psum | solution.py:9
  326.5 6.2 fusion.2
  332.8 4.2 exponential_reduce_fusion
  337.0 2.5 multiply_reduce_fusion.4
  340.5 0.9 copy.17
  341.7 4.3 convolution_bitcast_fusion
  346.0 1.2 copy.16
  347.3 6.3 fusion.15
  353.6 9.1 %fusion.36 = (f32[6,14,14,256]{3,2,1,0:T(8,128)S(1)}, f32[6,14,14,256]{3,2,1,0:T(8,128)}, f32[6,14,14,256]{3,2,1,0:T(8,128)}, f32[6,14,14,256]{3,2,1,0:T(8,128)}...) fusion(f32[6,14,14,2304]{3,2,1,0:T(8,128)} %fusion.15), kind=kLoop, calls=%fused_computation.104 | loop fusion | bytes 21676032 | tf_op jit(solution)/shard_map/slice | solution.py:28
  362.7 2.1 pad_add_fusion
  365.6 4.1 pad_add_fusion.1
  369.7 2.5 reshape.82
  372.2 5.0 convolution_bitcast_fusion.1
  377.2 1.2 copy.15
  378.5 6.5 pad_maximum_fusion
  386.2 268.4 %all-reduce.16.cloned.1.call-done = f32[1310720]{0:T(1024)} async-done(((f32[1310720]{0:T(1024)}), f32[1310720]{0:T(1024)}) %all-reduce.16.cloned.1.call-update) | async-done | bytes 5242896 | tf_op jit(solution)/shard_map/psum | solution.py:130
  654.6 1.8 multiply_reduce_fusion.3
  657.0 3.6 multiply_reduce_fusion.1
  661.9 1.1 slice_multiply_fusion.2
  663.0 2.7 slice_multiply_fusion.1
  (73 shorter events, 8.9 us)
Async XLA Ops:
  7.2 75.5 %copy-start = (bf16[3,3,256,256]{3,2,1,0:T(8,128)(2,1)S(1)}, bf16[3,3,256,256]{3,2,1,0:T(8,128)(2,1)}, u32[]{:S(2)}) copy-start(bf16[3,3,256,256]{3,2,1,0:T(8,128)(2,1)} %param.16) | copy-start | bytes 3538948
  7.2 26.8 %copy-start.2 = (bf16[6,14,14,256]{3,2,1,0:T(8,128)(2,1)S(1)}, bf16[6,14,14,256]{3,2,1,0:T(8,128)(2,1)}, u32[]{:S(2)}) copy-start(bf16[6,14,14,256]{3,2,1,0:T(8,128)(2,1)} %param.13) | copy-start | bytes 1806340
  7.2 319.3 %all-reduce.14.cloned.1.call-start = ((), (), s32[]{:S(2)}) async-start(), calls=%async_computation | async-start | bytes 1048576 | tf_op jit(solution)/shard_map/psum | solution.py:9
  33.9 620.7 %all-reduce.16.cloned.1.call-start = ((), (), s32[]{:S(2)}) async-start(), calls=%async_computation.1 | async-start | bytes 10485760 | tf_op jit(solution)/shard_map/psum | solution.py:130
  44.8 9.3 %copy-start.21 = (bf16[3,3,256,256]{3,2,1,0:T(8,128)(2,1)S(1)}, bf16[3,3,256,256]{3,2,1,0:T(8,128)(2,1)}, u32[]{:S(2)}) copy-start(bf16[3,3,256,256]{3,2,1,0:T(8,128)(2,1)} %param.15) | copy-start | bytes 3538948
  44.8 9.3 %copy-start.22 = (f32[256]{0:T(256)S(1)}, f32[256]{0:T(256)}, u32[]{:S(2)}) copy-start(f32[256]{0:T(256)} %param.17) | copy-start | bytes 3076
  59.3 0.8 copy-start.8
  77.9 3.5 copy-start.13
  78.9 2.4 copy-start.14
  78.9 2.5 copy-start.9
  80.1 1.4 copy-start.12
  81.3 1.1 copy-start.11
  81.4 1.1 copy-start.10
  81.5 3.5 copy-start.18
  82.6 2.3 copy-start.20
  87.7 1.5 copy-start.17
  87.7 1.6 copy-start.19
  93.9 238.9 %copy-start.23 = (s32[6]{0:T(128)S(1)}, s32[6]{0:T(128)}, u32[]{:S(2)}) copy-start(s32[6]{0:T(128)} %param.14) | copy-start | bytes 76
  332.7 7.1 %copy-start.16 = (bf16[2048,512]{1,0:T(8,128)(2,1)}, bf16[2048,512]{1,0:T(8,128)(2,1)S(1)}, u32[]{:S(2)}) copy-start(bf16[2048,512]{1,0:T(8,128)(2,1)S(1)} %get-tuple-element.9) | copy-start | bytes 6291460
  346.0 1.2 copy-start.7
  362.6 2.1 copy-start.3
  362.6 2.2 copy-start.4
  362.7 2.6 copy-start.5
  362.7 3.0 copy-start.6
  377.2 1.2 copy-start.15
  385.0 0.7 copy-start.24
  665.7 1.3 copy-start.1
Sparse Core Ops, SparseCore 0:
  34.0 292.4 all-reduce.13
  385.1 269.3 all-reduce.15
where the time goes:
time: 676 us; the launch traced here: 674 us
  waiting for transfers between devices  501 us (74%)
  local copies, waits for them, and re-layouts  65 us (10%)
  other arithmetic  33.2 us (5%)
  matrix products  31.6 us (5%)
  blocking collectives  25.1 us (4%)
  between operations  17.8 us (3%)
    psum x1, waiting for transfers between devices, shards(): summed = lax.psum(grad_flat, ('dp', 'rep'))  268 us
    psum x1, waiting for transfers between devices, spread(): return lax.psum(jnp.where(mine, value, jnp.zeros_like(value)), axis)  233 us
    all_gather x1, blocking collectives, shards(): group_panel = lax.all_gather(candidates, 'rep', axis=0, tiled=True)  25.1 us
    unnamed x69, local copies, waits for them, and re-layouts  20.9 us
    concatenate x10, local copies, waits for them, and re-layouts, patches_of(): return jnp.concatenate(shifted, axis=3)  13.6 us
  transfers between devices with their start and end apart: 2, of which 2 were waited for; matrix products, arithmetic and copies ran while one was open for 8% of the time, Pallas kernels for 0%

commit v1 on v0

v1 whole, which is shorter than its diff:
```python
import functools

import jax
import jax.numpy as jnp
from jax import lax
from jax.experimental import pallas as pl
from jax.experimental.pallas import tpu as pltpu
from jax.sharding import PartitionSpec as P

F32 = jnp.float32
BF16 = jnp.bfloat16
MESH = pl.DeviceIdType.MESH
VMEM = pltpu.VMEM
DMA = pltpu.SemaphoreType.DMA

IMG, SIDE, C, E = 6, 14, 256, 512
PAD = 16
CELLS = SIDE * PAD
TALL = 288
QUEUE, GEN = 2048, 512
ROWS = 5120
CONV_ROWS = 2304
CHUNK = 20

NN = (((1,), (0,)), ((), ()))
NT = (((1,), (1,)), ((), ()))
TN = (((0,), (0,)), ((), ()))


def dot(a, b, dims=NN):
    return lax.dot_general(a, b, dims, preferred_element_type=F32)


def place():
    dp, rep = lax.axis_index("dp"), lax.axis_index("rep")
    return dp // 8, (dp // 2) % 4, dp % 2, rep // 4, rep % 4


def peer(dz=0, dx=0, dc=0, dy=0, dlo=0):
    z_hi, x, core, z_lo, y = place()
    z = (z_hi * 2 + (z_lo + dlo) % 2 + dz) % 8
    x, y, core = (x + dx) % 4, (y + dy) % 4, (core + dc) % 2
    return ((z // 2) * 4 + x) * 2 + core, (z % 2) * 4 + y


def stack3(v):
    high = v.astype(BF16).astype(F32)
    rest = v - high
    mid = rest.astype(BF16).astype(F32)
    low = rest - mid
    return jnp.concatenate([high, mid, low, jnp.zeros_like(v)], axis=0).astype(BF16)


def dot3(v, b, dims=NN):
    n = v.shape[0]
    out = dot(stack3(v), b, dims)
    return out[:n] + out[n : 2 * n] + out[2 * n : 3 * n]


def row_lengths(rows):
    f = rows.astype(F32)
    sq = f * f
    high = sq.astype(BF16)
    low = (sq - high.astype(F32)).astype(BF16)
    ones = jnp.ones((16, rows.shape[1]), BF16)
    total = dot(ones, high, NT) + dot(ones, low, NT)
    return lax.rsqrt(total[:8] + 1e-06)


XY = [(dx, dy) for dx in range(4) for dy in range(4) if dx or dy]


def kernel(
    img_hbm,
    lab,
    one_hbm,
    two_hbm,
    slope,
    spatial,
    head,
    queue_hbm,
    cand,
    gen,
    off,
    loss_out,
    fresh_out,
    upd_out,
    img,
    w1,
    w2,
    w2t,
    qb,
    s1,
    s2,
    sd,
    sp,
    xt,
    ht,
    fac,
    spm,
    pooled,
    cm,
    c_rec,
    ch,
    x_rec,
    ch2,
    z_rec,
    half,
    pan,
    gb,
    r1,
    ta,
    tbf,
    tb,
    ra,
    rb,
    uaf,
    ua,
    ubf,
    ub,
    ra2,
    rb2,
    zsf,
    zs,
    zr,
    ns,
    nr1,
    nr2,
    nr3,
    ld_sem,
    pan_s,
    pan_r,
    core_s,
    core_r,
    grad_s,
    grad_r,
    z_s,
    z_r,
    n_s,
    n_r,
):
    z_hi, x_me, core, z_lo, y_me = place()
    dp, rep = lax.axis_index("dp"), lax.axis_index("rep")
    z_me = z_hi * 2 + z_lo
    first_row = (dp * 8 + rep) * CHUNK

    def remote(src, dst, s, r, to):
        return pltpu.make_async_remote_copy(
            src_ref=src,
            dst_ref=dst,
            send_sem=s,
            recv_sem=r,
            device_id=to,
            device_id_type=MESH,
        )

    loads = [
        pltpu.make_async_copy(a, b, ld_sem.at[k])
        for k, (a, b) in enumerate(
            [(img_hbm, img), (one_hbm, w1), (two_hbm, w2), (queue_hbm, qb)]
        )
    ]
    for cp in loads:
        cp.start()

    barrier = pltpu.get_barrier_semaphore()
    friends = [dict(dc=1)] + [dict(dx=a, dy=b) for a, b in XY]
    friends += [dict(dz=k) for k in range(1, 8)]
    friends += [dict(dlo=1, dy=k) for k in range(1, 4)]
    for f in friends:
        pl.semaphore_signal(barrier, inc=1, device_id=peer(**f), device_id_type=MESH)

    mine = jnp.where(gen[0] == dp, 1.0, 0.0)
    cm[...] = (cand[...].astype(F32) * mine).astype(BF16)
    for buf in (s1, s2, sd, sp):
        for b in range(IMG):
            buf[b, 0:16, :] = jnp.zeros((16, 3 * C), BF16)
            buf[b, 240:TALL, :] = jnp.zeros((TALL - 240, 3 * C), BF16)
    pooled[...] = jnp.zeros((8, C), F32)

    pl.semaphore_wait(barrier, len(friends))

    other_half = cm.at[pl.ds(pl.multiple_of((1 - core) * 32, 32), 32)]
    p_core = remote(other_half, c_rec, pan_s.at[0], pan_r.at[0], peer(dc=1))
    p_core.start()

    quarter = lax.broadcasted_iota(jnp.int32, (CELLS, C), 0) % PAD
    inside = quarter < SIDE

    def shifted(buf, b, v):
        buf[b, 16:240, 0:C] = pltpu.roll(v, 1, 0).astype(BF16)
        buf[b, 16:240, C : 2 * C] = v.astype(BF16)
        buf[b, 16:240, 2 * C : 3 * C] = pltpu.roll(v, CELLS - 1, 0).astype(BF16)

    def flip(buf, b, v):
        tall = jnp.concatenate([v, jnp.zeros((32, C), F32)], axis=0)
        buf[:, pl.ds(pl.multiple_of(b * 256, 256), 256)] = tall.T.astype(BF16)

    loads[0].wait()

    def prepare(b, _):
        v = img[b].astype(F32)
        v = jnp.concatenate([v, jnp.zeros((SIDE, PAD - SIDE, C), F32)], axis=1)
        v = v.reshape(CELLS, C)
        shifted(s1, b, v)
        flip(xt, b, v)
        return 0

    lax.fori_loop(0, IMG, prepare, 0)

    p_core.wait()
    own_half = cm[pl.ds(pl.multiple_of(core * 32, 32), 32)]
    ch[...] = (own_half.astype(F32) + c_rec[...].astype(F32)).astype(BF16)
    p_x = [
        remote(ch, x_rec.at[k - 1], pan_s.at[k], pan_r.at[k], peer(dx=k))
        for k in (1, 3, 2)
    ]
    for cp in p_x:
        cp.start()

    loads[1].wait()

    def conv(buf, w, b):
        out = dot(buf[b, 0:CELLS], w[0].reshape(3 * C, C))
        out += dot(buf[b, 16 : 16 + CELLS], w[1].reshape(3 * C, C))
        return out + dot(buf[b, 32 : 32 + CELLS], w[2].reshape(3 * C, C))

    def first(b, _):
        pre = conv(s1, w1, b)
        f = jnp.where(inside, jnp.where(pre > 0, 1.0, slope[...]), 0.0)
        fac[b] = f
        h = pre * f
        shifted(s2, b, h)
        flip(ht, b, h)
        return 0

    lax.fori_loop(0, IMG, first, 0)

    for cp in p_x:
        cp.wait()
    whole = ch[...].astype(F32)
    for k in range(3):
        whole += x_rec[k].astype(F32)
    ch2[...] = whole.astype(BF16)
    p_z = [
        remote(ch2, z_rec.at[k - 1], pan_s.at[3 + k], pan_r.at[3 + k], peer(dz=2 * k))
        for k in (1, 3, 2)
    ]
    for cp in p_z:
        cp.start()

    for p in range(SIDE):
        spm[1, p * PAD : p * PAD + SIDE, :] = spatial[p * SIDE : (p + 1) * SIDE, :]
        spm[1, p * PAD + SIDE : (p + 1) * PAD, :] = jnp.zeros((PAD - SIDE, C), F32)
    loads[2].wait()

    def second(b, _):
        out = conv(s2, w2, b) + s1[b, 16:240, C : 2 * C].astype(F32)
        pooled[pl.ds(b, 1), :] = jnp.sum(out * spm[1], axis=0, keepdims=True)
        return 0

    lax.fori_loop(0, IMG, second, 0)

    for cp in p_z:
        cp.wait()
    whole = ch2[...].astype(F32)
    for k in range(3):
        whole += z_rec[k].astype(F32)
    half[rep] = whole.astype(BF16)
    rep_moves = [(lo, dy) for lo in range(2) for dy in range(4) if lo or dy]
    p_rep = [
        remote(
            half.at[rep],
            half.at[rep],
            pan_s.at[7 + k],
            pan_r.at[7 + k],
            peer(dlo=lo, dy=dy),
        )
        for k, (lo, dy) in enumerate(rep_moves)
    ]
    for cp in p_rep:
        cp.start()

    spm[0] = pltpu.roll(spm[1], 1, 0)
    spm[2] = pltpu.roll(spm[1], CELLS - 1, 0)
    for r in range(3):
        for s in range(3):
            turned = w2[2 - r, 2 - s].astype(F32).T
            w2t[r, s] = turned.astype(BF16)

    po = pooled[...]
    embed = dot3(po, head[...])
    inv_len = lax.rsqrt(jnp.sum(embed * embed, axis=1, keepdims=True) + 1e-06)
    unit = embed * inv_len
    rows8 = lax.broadcasted_iota(jnp.int32, (8, 1), 0)
    labels = jnp.full((8, 1), -1, jnp.int32)
    for b in range(IMG):
        labels = jnp.where(rows8 == b, lab[b], labels)
    shift = off[0]

    loads[3].wait()

    def score(rows, slots, keep):
        scale = row_lengths(rows)
        hot = (labels == slots) & keep
        logits = 64.0 * (dot3(unit, rows, NT) * scale - jnp.where(hot, 0.4, 0.0))
        exps = jnp.where(keep, jnp.exp(logits), 0.0)
        total = jnp.sum(exps, axis=1, keepdims=True)
        at_label = jnp.sum(jnp.where(hot, logits, 0.0), axis=1, keepdims=True)
        pulls = jnp.concatenate([exps * scale, jnp.where(hot, scale, 0.0)], axis=0)
        return total, at_label, dot3(pulls, rows)

    total = jnp.zeros((8, 1), F32)
    at_label = jnp.zeros((8, 1), F32)
    pulled = jnp.zeros((16, E), F32)
    for k in range(4):
        rows = qb[k * 512 : (k + 1) * 512, :]
        slots = lax.broadcasted_iota(jnp.int32, (8, 512), 1) + k * 512
        fresh = ((slots - shift + QUEUE) & (QUEUE - 1)) < GEN
        t, a, u = score(rows, slots, jnp.logical_not(fresh))
        total, at_label, pulled = total + t, at_label + a, pulled + u

    for cp in p_rep:
        cp.wait()
    my_rows = pl.ds(pl.multiple_of(core * 32, 32), 32)
    pan[:, my_rows, :] = half[...]
    p_last = remote(half, pan.at[:, my_rows, :], pan_s.at[14], pan_r.at[14], peer(dc=1))
    p_last.start()
    p_last.wait()

    rows = pan[...].reshape(GEN, E)
    j = lax.broadcasted_iota(jnp.int32, (8, GEN), 1)
    t, a, u = score(rows, (j + shift) & (QUEUE - 1), j >= 0)
    total, at_label, pulled = total + t, at_label + a, pulled + u
    loss = jnp.log(total) - at_label
    lanes = lax.broadcasted_iota(jnp.int32, (8, 128), 1)
    rows128 = lax.broadcasted_iota(jnp.int32, (8, 128), 0)
    loss_out[...] = jnp.sum(
        jnp.where(lanes == rows128, loss, 0.0), axis=0, keepdims=True
    )
    d_unit = 64.0 * (pulled[0:8] / total - pulled[8:16])
    d_embed = (d_unit - unit * jnp.sum(d_unit * unit, axis=1, keepdims=True)) * inv_len
    d_embed = jnp.where(rows8 < IMG, d_embed, 0.0)
    d_pooled = dot3(d_embed, head[...], NT)

    for b in range(IMG):
        for s in range(3):
            sd[b, 16:240, s * C : (s + 1) * C] = (
                spm[s] * d_pooled[b : b + 1, :]
            ).astype(BF16)

    po_h = po.astype(BF16).astype(F32)
    de_h = d_embed.astype(BF16).astype(F32)
    left = jnp.concatenate([po_h, po_h, po - po_h, jnp.zeros_like(po)], axis=0)
    right = jnp.concatenate(
        [de_h, d_embed - de_h, de_h, jnp.zeros_like(d_embed)], axis=0
    )
    g_head = dot(left.T.astype(BF16), right.astype(BF16))
    zsf2 = tbf.reshape(1280, 128)
    for k in range(2):
        for h in range(2):
            zsf2[pl.ds(k * 512 + h, 256, stride=2), :] = g_head[
                :, h * 256 + k * 128 : h * 256 + (k + 1) * 128
            ]
    for k in range(2):
        gb[2 * CONV_ROWS :, k * 128 : (k + 1) * 128] = zsf2[
            k * 512 : (k + 1) * 512, :
        ].astype(BF16)

    def weight_grad(turned, buf, tap, base):
        r, s = 2 - tap // 3, 2 - tap % 3
        rows = buf[:, r * 16 : r * 16 + 256, s * C : (s + 1) * C].reshape(IMG * 256, C)
        gb[base + tap * 256 : base + (tap + 1) * 256, :] = dot(turned[...], rows).astype(
            BF16
        )

    def core_send(a):
        theirs = pl.ds(pl.multiple_of((2 * a + 1 - core) * 160, 32), 160)
        cp = remote(
            gb.at[theirs],
            r1.at[pl.ds(a * 160, 160)],
            core_s.at[a],
            core_r.at[a],
            peer(dc=1),
        )
        cp.start()
        return cp

    core_cps = [None] * 16
    for tap in range(9):
        weight_grad(ht, sd, tap, CONV_ROWS)
        for a in range(8, 16):
            if core_cps[a] is None and (a + 1) * 320 <= CONV_ROWS + (tap + 1) * 256:
                core_cps[a] = core_send(a)
    for a in range(8, 16):
        if core_cps[a] is None:
            core_cps[a] = core_send(a)

    def back(b, _):
        out = conv(sd, w2t, b) * fac[b]
        shifted(sp, b, out)
        return 0

    lax.fori_loop(0, IMG, back, 0)

    def after_core(g):
        for a in range(8 * g, 8 * g + 8):
            core_cps[a].wait()

        def add(i, _):
            a = 8 * g + i
            ours = pl.ds(pl.multiple_of((2 * a + core) * 160, 32), 160)
            v = gb[ours, :].astype(F32)
            v += r1[pl.ds(pl.multiple_of(a * 160, 32), 160), :].astype(F32)
            ta[a] = v[:, 0:128].astype(BF16)
            for lo in range(2):
                for y in range(4):
                    at = pl.multiple_of(i * 40, 8)
                    k = (lo * 4 + y) * CHUNK
                    tbf[y, pl.ds(at + lo * CHUNK, CHUNK), :] = v[k : k + CHUNK, 128:256]
            return 0

        lax.fori_loop(0, 8, add, 0)
        for y in range(4):
            tb[g, y] = tbf[y].astype(BF16)
        cps = []
        for k in (1, 3, 2):
            to = (x_me + k) % 4
            n = g * 9 + (k - 1) * 3
            for h in range(2):
                cps.append(
                    remote(
                        ta.at[8 * g + 4 * h + to],
                        ra.at[g, k - 1, h],
                        grad_s.at[n + h],
                        grad_r.at[n + h],
                        peer(dx=k),
                    )
                )
            cps.append(
                remote(
                    tb.at[g, (y_me + k) % 4],
                    rb.at[g, k - 1],
                    grad_s.at[n + 2],
                    grad_r.at[n + 2],
                    peer(dy=k),
                )
            )
        for cp in cps:
            cp.start()
        return cps

    def after_first(g, cps):
        for cp in cps:
            cp.wait()
        for h in range(2):
            v = ta[8 * g + 4 * h + x_me].astype(F32)
            for k in range(3):
                v += ra[g, k, h].astype(F32)
            for lo in range(2):
                for y in range(4):
                    k = (lo * 4 + y) * CHUNK
                    at = (h * 2 + lo) * CHUNK
                    uaf[y, at : at + CHUNK, :] = v[k : k + CHUNK]
        v = tb[g, y_me].astype(F32)
        for k in range(3):
            v += rb[g, k].astype(F32)
        for h in range(2):
            for x in range(4):
                k = (h * 4 + x) * 40
                ubf[x, h * 40 : h * 40 + 40, :] = v[k : k + 40]
        ua[g] = uaf[...].astype(BF16)
        ub[g] = ubf[...].astype(BF16)
        cps = []
        for k in (1, 3, 2):
            n = 18 + g * 6 + (k - 1) * 2
            cps.append(
                remote(
                    ua.at[g, (y_me + k) % 4],
                    ra2.at[g, k - 1],
                    grad_s.at[n],
                    grad_r.at[n],
                    peer(dy=k),
                )
            )
            cps.append(
                remote(
                    ub.at[g, (x_me + k) % 4],
                    rb2.at[g, k - 1],
                    grad_s.at[n + 1],
                    grad_r.at[n + 1],
                    peer(dx=k),
                )
            )
        for cp in cps:
            cp.start()
        return cps

    def after_second(g, cps):
        for cp in cps:
            cp.wait()
        for side, (own, rec) in enumerate(((ua[g, y_me], ra2), (ub[g, x_me], rb2))):
            v = own.astype(F32)
            for k in range(3):
                v += rec[g, k].astype(F32)
            for z in range(4):
                zsf[4 * g + z, side * CHUNK : (side + 1) * CHUNK, :] = v[
                    z * CHUNK : (z + 1) * CHUNK
                ]

    early = after_core(1)
    for tap in range(9):
        weight_grad(xt, sp, tap, 0)
        for a in range(8):
            done = (tap + 1) * 256 + (256 if tap == 8 else 0)
            if core_cps[a] is None and (a + 1) * 320 <= done:
                core_cps[a] = core_send(a)
    early = after_first(1, early)
    late = after_core(0)

    def renew(k, _):
        at = pl.ds(pl.multiple_of(k * 256, 256), 256)
        slot = lax.broadcasted_iota(jnp.int32, (256, GEN), 0) + k * 256
        source = (slot - shift + QUEUE) & (QUEUE - 1)
        pick = jnp.where(
            source == lax.broadcasted_iota(jnp.int32, (256, GEN), 1), 1.0, 0.0
        ).astype(BF16)
        new = dot(pick, pan[...].reshape(GEN, E))
        old = qb[at, :].astype(F32)
        qb[at, :] = jnp.where(source < GEN, new, old).astype(BF16)
        return 0

    lax.fori_loop(0, QUEUE // 256, renew, 0)
    store = pltpu.make_async_copy(qb, fresh_out, ld_sem.at[4])
    store.start()

    after_second(1, early)
    late = after_first(0, late)
    after_second(0, late)

    for z in range(8):
        zsf[z, 40:48, :] = jnp.zeros((8, 128), F32)
        zs[z] = zsf[z].astype(BF16)
    z_cps = [
        remote(zs.at[(z_me + k) % 8], zr.at[k - 1], z_s.at[k - 1], z_r.at[k - 1], peer(dz=k))
        for k in (1, 7, 2, 6, 3, 5, 4)
    ]
    for cp in z_cps:
        cp.start()
    for cp in z_cps:
        cp.wait()
    v = zsf[z_me]
    for k in range(7):
        v += zr[k].astype(F32)
    low, high = v[0:CHUNK], v[CHUNK : 2 * CHUNK]

    row = first_row + lax.broadcasted_iota(jnp.int32, (CHUNK, 128), 0)
    in_one = row < CONV_ROWS
    in_head = row >= 2 * CONV_ROWS
    in_two = jnp.logical_not(in_one | in_head)
    sq = low * low + high * high
    for k, m in enumerate((in_one, in_two, in_head)):
        ns[0, k : k + 1, :] = jnp.sum(jnp.where(m, sq, 0.0), axis=0, keepdims=True)
    ns[0, 3:8, :] = jnp.zeros((5, 128), F32)

    def gather_sums(level, dst, moves, base):
        cps = [
            remote(ns.at[level], dst.at[k], n_s.at[base + k], n_r.at[base + k], peer(**m))
            for k, m in enumerate(moves)
        ]
        for cp in cps:
            cp.start()
        for cp in cps:
            cp.wait()
        s = ns[level]
        for k in range(len(moves)):
            s += dst[k]
        return s

    ns[1] = gather_sums(0, nr1, [dict(dx=a, dy=b) for a, b in XY], 0)
    ns[2] = gather_sums(1, nr2, [dict(dz=k) for k in range(1, 8)], 15)
    s = gather_sums(2, nr3, [dict(dc=1)], 22)
    s = jnp.sum(s, axis=1, keepdims=True)
    scale = lax.rsqrt(s + 1e-06)
    conv_n, head_n = (9 * C * C) ** 0.5, (C * E) ** 0.5
    factor = jnp.where(
        in_one,
        scale[0:1] * conv_n,
        jnp.where(in_two, scale[1:2] * conv_n, scale[2:3] * head_n),
    )
    upd_out[pl.ds(0, CHUNK, stride=2), :] = low * factor
    upd_out[pl.ds(1, CHUNK, stride=2), :] = high * factor
    store.wait()


SCRATCH = [
    VMEM((IMG, SIDE, SIDE, C), BF16),
    VMEM((3, 3, C, C), BF16),
    VMEM((3, 3, C, C), BF16),
    VMEM((3, 3, C, C), BF16),
    VMEM((QUEUE, E), BF16),
    VMEM((IMG, TALL, 3 * C), BF16),
    VMEM((IMG, TALL, 3 * C), BF16),
    VMEM((IMG, TALL, 3 * C), BF16),
    VMEM((IMG, TALL, 3 * C), BF16),
    VMEM((C, IMG * 256), BF16),
    VMEM((C, IMG * 256), BF16),
    VMEM((IMG, CELLS, C), F32),
    VMEM((3, CELLS, C), F32),
    VMEM((8, C), F32),
    VMEM((64, E), BF16),
    VMEM((32, E), BF16),
    VMEM((32, E), BF16),
    VMEM((3, 32, E), BF16),
    VMEM((32, E), BF16),
    VMEM((3, 32, E), BF16),
    VMEM((8, 32, E), BF16),
    VMEM((8, 64, E), BF16),
    VMEM((ROWS, C), BF16),
    VMEM((ROWS // 2, C), BF16),
    VMEM((16, 160, 128), BF16),
    VMEM((4, 320, 128), F32),
    VMEM((2, 4, 320, 128), BF16),
    VMEM((2, 3, 2, 160, 128), BF16),
    VMEM((2, 3, 320, 128), BF16),
    VMEM((4, 80, 128), F32),
    VMEM((2, 4, 80, 128), BF16),
    VMEM((4, 80, 128), F32),
    VMEM((2, 4, 80, 128), BF16),
    VMEM((2, 3, 80, 128), BF16),
    VMEM((2, 3, 80, 128), BF16),
    VMEM((8, 48, 128), F32),
    VMEM((8, 48, 128), BF16),
    VMEM((7, 48, 128), BF16),
    VMEM((3, 8, 128), F32),
    VMEM((15, 8, 128), F32),
    VMEM((7, 8, 128), F32),
    VMEM((1, 8, 128), F32),
    DMA((5,)),
    DMA((15,)),
    DMA((15,)),
    DMA((16,)),
    DMA((16,)),
    DMA((30,)),
    DMA((30,)),
    DMA((7,)),
    DMA((7,)),
    DMA((23,)),
    DMA((23,)),
]


def shards(
    images,
    labels,
    conv_one,
    conv_two,
    prelu_slope,
    spatial,
    head_weight,
    class_queue,
    candidates,
    generator,
    offset,
):
    far = pl.BlockSpec(memory_space=pl.ANY)
    near = pl.BlockSpec(memory_space=pltpu.VMEM)
    scalar = pl.BlockSpec(memory_space=pltpu.SMEM)
    loss, fresh, update = pl.pallas_call(
        kernel,
        out_shape=(
            jax.ShapeDtypeStruct((1, 128), F32),
            jax.ShapeDtypeStruct((QUEUE, E), BF16),
            jax.ShapeDtypeStruct((2 * CHUNK, 128), F32),
        ),
        in_specs=[far, scalar, far, far, near, near, near, far, near, scalar, scalar],
        out_specs=(near, far, near),
        scratch_shapes=SCRATCH,
        name="whole_step",
        compiler_params=pltpu.CompilerParams(
            collective_id=0, has_side_effects=True, vmem_limit_bytes=56 << 20
        ),
    )(
        images,
        labels,
        conv_one,
        conv_two,
        prelu_slope.reshape(1, C),
        spatial,
        head_weight,
        class_queue,
        candidates,
        generator,
        offset,
    )
    return loss[0, :IMG], fresh, update.reshape(2 * CHUNK * 128)


def solution(mesh):
    in_specs = (
        P(("dp", "rep"), None, None, None),
        P(("dp", "rep")),
        P(),
        P(),
        P(),
        P(),
        P(),
        P(),
        P(("dp", "rep"), None),
        P(),
        P(),
    )
    out_specs = (P(("dp", "rep")), P(), P(("dp", "rep")))
    return jax.shard_map(
        shards, mesh=mesh, in_specs=in_specs, out_specs=out_specs, check_vma=False
    )
```

time: 676 us -> 79.2 us (0.12)
  waiting for transfers between devices: 501 us -> 0 us
  Pallas kernels: 0 us -> 72.9 us
  local copies, waits for them, and re-layouts: 65 us -> 4.84 us
  other arithmetic: 33.2 us -> 0 us
  matrix products: 31.6 us -> 0 us
  blocking collectives: 25.1 us -> 0 us
  between operations: 17.8 us -> 1.29 us
    psum x2 -> x0, waiting for transfers between devices: 501 us -> none  [the longest x1 268 us: shards(): summed = lax.psum(grad_flat, ('dp', 'rep'))]
    pallas_call x0 -> x1, Pallas kernels: none -> 72.9 us  [shards(): pl.pallas_call(kernel, out_shape=(jax.ShapeDtypeStruct((1, 128), F32), ja...]
    dot_general x10 -> x0, matrix products: 31.6 us -> none  [the longest x1 6.33 us: local_step(): jnp.dot(d_block, w_two.T, preferred_element_type=jnp.float32)]
    all_gather x1 -> x0, blocking collectives: 25.1 us -> none  [shards(): group_panel = lax.all_gather(candidates, 'rep', axis=0, tiled=True)]
    unnamed x69 -> x4, local copies, waits for them, and re-layouts: 20.9 us -> 3.67 us
    slice x2 -> x0, local copies, waits for them, and re-layouts: 14.3 us -> none  [the longest x1 9.06 us: fold_back(): tap_block = grad_patch[..., tap_index * channels:(tap_index + 1) * channels]]
    reshape x4 -> x0, local copies, waits for them, and re-layouts: 14.3 us -> none  [the longest x1 9.31 us: local_step(): patch_one = patches_of(images).reshape(cell_count, 9 * channels)]
    concatenate x10 -> x0, local copies, waits for them, and re-layouts: 13.6 us -> none  [patches_of(): return jnp.concatenate(shifted, axis=3)]
  transfers between devices with their start and end apart: 2 -> 0, of which waited for: 2 -> 0; matrix products, arithmetic and copies ran while one was open for 8% -> 0% of each run, Pallas kernels for 0% -> 0%
where the time goes in v1:
time: 79.2 us; the launch traced here: 79 us
  Pallas kernels  72.9 us (92%)
  local copies, waits for them, and re-layouts  4.84 us (6%)
  between operations  1.29 us (2%)
    pallas_call x1, Pallas kernels, shards(): pl.pallas_call(kernel, out_shape=(jax.ShapeDtypeStruct((1, 128), F32), ja...  72.9 us
    unnamed x4, local copies, waits for them, and re-layouts  3.67 us

profile of v1, /device:TPU:1, one launch (start us, length us, event | category | flops | bytes accessed | tf_op | source)
XLA Modules:
  0.0 79.0 jit_solution(13758526005577356321)
XLA Ops:
  1.3 72.9 %whole_step.1 = (f32[1,128]{1,0:T(1,128)}, bf16[2048,512]{1,0:T(8,128)(2,1)}, f32[40,128]{1,0:T(8,128)}) custom-call(bf16[6,14,14,256]{3,2,1,0:T(8,128)(2,1)} %img_hbm.1, s32[6]{0:T(128)} %lab.1, bf16[3,3,256,256]{3,2,1,0:T(8,128)(2,1)} %one_hbm.1, bf16[3,3,256,256]{3,2,1,0:T(8,128)(2,1)} %two_hbm.1, f32[1,256]{1,0:T(1,128)} %bitcast.5, f32[196,256]{1,0:T(8,128)} %spatial.1, ...), custom_call_target="tpu_custom_call" | custom-call | tf_op jit(solution)/shard_map/whole_step/pallas_call | solution.py:669
  74.2 1.2 %slice_bitcast_fusion = f32[6]{0:T(128)} fusion(f32[1,128]{1,0:T(1,128)} %get-tuple-element.6), kind=kLoop, calls=%fused_computation | loop fusion | bytes 48 | tf_op jit(solution)/shard_map/squeeze | solution.py:696
  75.4 0.0 copy-start
  75.4 3.1 %copy.17 = bf16[2048,512]{1,0:T(8,128)(2,1)} copy(bf16[2048,512]{1,0:T(8,128)(2,1)} %get-tuple-element.13) | data formatting | bytes 4194304
  78.4 0.0 copy-done
  78.4 0.6 copy.18
Async XLA Ops:
  75.4 3.1 %copy-start = (f32[40,128]{1,0:T(8,128)S(1)}, f32[40,128]{1,0:T(8,128)}, u32[]{:S(2)}) copy-start(f32[40,128]{1,0:T(8,128)} %get-tuple-element.8) | copy-start | bytes 61444

commit v2 on v1

v2 whole, which is shorter than its diff:
```python
import functools

import jax
import jax.numpy as jnp
from jax import lax
from jax.experimental import pallas as pl
from jax.experimental.pallas import tpu as pltpu
from jax.sharding import PartitionSpec as P

F32 = jnp.float32
BF16 = jnp.bfloat16
MESH = pl.DeviceIdType.MESH
VMEM = pltpu.VMEM
DMA = pltpu.SemaphoreType.DMA

IMG, SIDE, C, E = 6, 14, 256, 512
PAD = 16
CELLS = SIDE * PAD
TALL = 288
QUEUE, GEN = 2048, 512
ROWS = 5120
CONV_ROWS = 2304
CHUNK = 20

NN = (((1,), (0,)), ((), ()))
NT = (((1,), (1,)), ((), ()))
TN = (((0,), (0,)), ((), ()))


def dot(a, b, dims=NN):
    return lax.dot_general(a, b, dims, preferred_element_type=F32)


def place():
    dp, rep = lax.axis_index("dp"), lax.axis_index("rep")
    return dp // 8, (dp // 2) % 4, dp % 2, rep // 4, rep % 4


def peer(dz=0, dx=0, dc=0, dy=0, dlo=0):
    z_hi, x, core, z_lo, y = place()
    z = (z_hi * 2 + (z_lo + dlo) % 2 + dz) % 8
    x, y, core = (x + dx) % 4, (y + dy) % 4, (core + dc) % 2
    return ((z // 2) * 4 + x) * 2 + core, (z % 2) * 4 + y


def stack3(v):
    high = v.astype(BF16).astype(F32)
    rest = v - high
    mid = rest.astype(BF16).astype(F32)
    low = rest - mid
    return jnp.concatenate([high, mid, low, jnp.zeros_like(v)], axis=0).astype(BF16)


def dot3(v, b, dims=NN):
    n = v.shape[0]
    out = dot(stack3(v), b, dims)
    return out[:n] + out[n : 2 * n] + out[2 * n : 3 * n]


def row_lengths(rows):
    f = rows.astype(F32)
    sq = f * f
    high = sq.astype(BF16)
    low = (sq - high.astype(F32)).astype(BF16)
    ones = jnp.ones((16, rows.shape[1]), BF16)
    total = dot(ones, high, NT) + dot(ones, low, NT)
    return lax.rsqrt(total[:8] + 1e-06)


XY = [(dx, dy) for dx in range(4) for dy in range(4) if dx or dy]


def kernel(
    img_hbm,
    lab_hbm,
    one_hbm,
    two_hbm,
    slope_hbm,
    spatial_hbm,
    head_hbm,
    queue_hbm,
    cand_hbm,
    gen_hbm,
    off_hbm,
    loss_out,
    fresh_out,
    upd_out,
    lab,
    gen,
    off,
    slope,
    spatial,
    head,
    cand,
    img,
    w1,
    w2,
    w2t,
    qb,
    s1,
    s2,
    sd,
    sp,
    xt,
    ht,
    fac,
    spm,
    pooled,
    cm,
    c_rec,
    ch,
    x_rec,
    ch2,
    z_rec,
    half,
    pan,
    gb,
    r1,
    ta,
    tbf,
    tb,
    ra,
    uaf,
    ua,
    ubf,
    ub,
    ra2,
    zsf,
    zs,
    zr,
    ns,
    nr1,
    nr2,
    nr3,
    hgf,
    ld_sem,
    sem,
    rep_sem,
    core_sem,
    first_sem,
    second_sem,
):
    z_hi, x_me, core, z_lo, y_me = place()
    dp, rep = lax.axis_index("dp"), lax.axis_index("rep")
    z_me = z_hi * 2 + z_lo
    first_row = (dp * 8 + rep) * CHUNK

    def remote(src, dst, s, r, to):
        return pltpu.make_async_remote_copy(
            src_ref=src,
            dst_ref=dst,
            send_sem=s,
            recv_sem=r,
            device_id=to,
            device_id_type=MESH,
        )

    def wait_bytes(ref, sem):
        pltpu.make_async_copy(ref, ref, sem).wait()

    pairs = dict(
        cand=(cand_hbm, cand),
        gen=(gen_hbm, gen),
        img=(img_hbm, img),
        w1=(one_hbm, w1),
        slope=(slope_hbm, slope),
        w2=(two_hbm, w2),
        spatial=(spatial_hbm, spatial),
        head=(head_hbm, head),
        lab=(lab_hbm, lab),
        off=(off_hbm, off),
        queue=(queue_hbm, qb),
    )
    loads = {
        name: pltpu.make_async_copy(a, b, ld_sem.at[k])
        for k, (name, (a, b)) in enumerate(pairs.items())
    }
    for cp in loads.values():
        cp.start()

    barrier = pltpu.get_barrier_semaphore()
    friends = [dict(dc=1)] + [dict(dx=a, dy=b) for a, b in XY]
    friends += [dict(dz=k) for k in range(1, 8)]
    friends += [dict(dlo=1, dy=k) for k in range(1, 4)]
    for f in friends:
        pl.semaphore_signal(barrier, inc=1, device_id=peer(**f), device_id_type=MESH)

    loads["cand"].wait()
    loads["gen"].wait()
    mine = jnp.where(gen[0] == dp, 1.0, 0.0)
    cm[...] = (cand[...].astype(F32) * mine).astype(BF16)
    pl.semaphore_wait(barrier, len(friends))

    other_half = cm.at[pl.ds(pl.multiple_of((1 - core) * 32, 32), 32)]
    p_core = remote(other_half, c_rec, sem.at[0], sem.at[1], peer(dc=1))
    p_core.start()

    for buf in (s1, s2, sd, sp):
        for b in range(IMG):
            buf[b, 0:16, :] = jnp.zeros((16, 3 * C), BF16)
            buf[b, 240:TALL, :] = jnp.zeros((TALL - 240, 3 * C), BF16)
    pooled[...] = jnp.zeros((8, C), F32)
    uaf[...] = jnp.zeros((4, 48, 128), F32)
    ubf[...] = jnp.zeros((4, 48, 128), F32)
    zsf[...] = jnp.zeros((8, 48, 128), F32)

    quarter = lax.broadcasted_iota(jnp.int32, (2 * CELLS, C), 0) % PAD
    inside = quarter < SIDE

    def shifted(buf, b, v):
        before, after = pltpu.roll(v, 1, 0), pltpu.roll(v, 2 * CELLS - 1, 0)
        for k in range(2):
            part = slice(k * CELLS, (k + 1) * CELLS)
            buf[b + k, 16:240, 0:C] = before[part].astype(BF16)
            buf[b + k, 16:240, C : 2 * C] = v[part].astype(BF16)
            buf[b + k, 16:240, 2 * C : 3 * C] = after[part].astype(BF16)

    def flip(buf, b, v):
        for k in range(2):
            part = v[k * CELLS : (k + 1) * CELLS]
            tall = jnp.concatenate([part, jnp.zeros((32, C), F32)], axis=0)
            at = pl.ds(pl.multiple_of((b + k) * 256, 256), 256)
            buf[:, at] = tall.T.astype(BF16)

    loads["img"].wait()

    def prepare(i, _):
        b = 2 * i
        v = img[pl.ds(b, 2)].astype(F32)
        v = jnp.concatenate([v, jnp.zeros((2, SIDE, PAD - SIDE, C), F32)], axis=2)
        v = v.reshape(2 * CELLS, C)
        shifted(s1, b, v)
        flip(xt, b, v)
        return 0

    lax.fori_loop(0, IMG // 2, prepare, 0)

    p_core.wait_recv()
    own_half = cm[pl.ds(pl.multiple_of(core * 32, 32), 32)]
    ch[...] = (own_half.astype(F32) + c_rec[...].astype(F32)).astype(BF16)
    for k in (1, 3, 2):
        remote(ch, x_rec.at[k - 1], sem.at[2], sem.at[3], peer(dx=k)).start()

    loads["w1"].wait()
    loads["slope"].wait()

    def conv(buf, w, b):
        out = None
        for r in range(3):
            rows = buf[pl.ds(b, 2), r * 16 : r * 16 + CELLS, :]
            term = dot(rows.reshape(2 * CELLS, 3 * C), w[r].reshape(3 * C, C))
            out = term if out is None else out + term
        return out

    def first(i, _):
        b = 2 * i
        pre = conv(s1, w1, b)
        f = jnp.where(inside, jnp.where(pre > 0, 1.0, slope[...]), 0.0)
        fac[pl.ds(b, 2)] = f.reshape(2, CELLS, C)
        h = pre * f
        shifted(s2, b, h)
        flip(ht, b, h)
        return 0

    lax.fori_loop(0, IMG // 2, first, 0)

    wait_bytes(x_rec, sem.at[3])
    whole = ch[...].astype(F32)
    for k in range(3):
        whole += x_rec[k].astype(F32)
    ch2[...] = whole.astype(BF16)
    for k in (1, 3, 2):
        remote(ch2, z_rec.at[k - 1], sem.at[4], sem.at[5], peer(dz=2 * k)).start()

    loads["spatial"].wait()
    for p in range(SIDE):
        spm[1, p * PAD : p * PAD + SIDE, :] = spatial[p * SIDE : (p + 1) * SIDE, :]
        spm[1, p * PAD + SIDE : (p + 1) * PAD, :] = jnp.zeros((PAD - SIDE, C), F32)
    loads["w2"].wait()

    def second(i, _):
        b = 2 * i
        out = conv(s2, w2, b)
        for k in range(2):
            part = out[k * CELLS : (k + 1) * CELLS]
            part += s1[b + k, 16:240, C : 2 * C].astype(F32)
            pooled[pl.ds(b + k, 1), :] = jnp.sum(part * spm[1], axis=0, keepdims=True)
        return 0

    lax.fori_loop(0, IMG // 2, second, 0)

    wait_bytes(z_rec, sem.at[5])
    whole = ch2[...].astype(F32)
    for k in range(3):
        whole += z_rec[k].astype(F32)
    half[rep] = whole.astype(BF16)
    rep_moves = [(lo, dy) for lo in range(2) for dy in range(4) if lo or dy]
    for k, (lo, dy) in enumerate(rep_moves):
        to = peer(dlo=lo, dy=dy)
        remote(half.at[rep], half.at[rep], sem.at[6], rep_sem.at[k], to).start()

    spm[0] = pltpu.roll(spm[1], 1, 0)
    spm[2] = pltpu.roll(spm[1], CELLS - 1, 0)
    for r in range(3):
        for s in range(3):
            turned = w2[2 - r, 2 - s].astype(F32).T
            w2t[r, s] = turned.astype(BF16)

    for name in ("head", "lab", "off", "queue"):
        loads[name].wait()
    po = pooled[...]
    embed = dot3(po, head[...])
    inv_len = lax.rsqrt(jnp.sum(embed * embed, axis=1, keepdims=True) + 1e-06)
    unit = embed * inv_len
    rows8 = lax.broadcasted_iota(jnp.int32, (8, 1), 0)
    labels = jnp.full((8, 1), -1, jnp.int32)
    for b in range(IMG):
        labels = jnp.where(rows8 == b, lab[b], labels)
    shift = off[0]

    def score(rows, slots, keep):
        scale = row_lengths(rows)
        hot = (labels == slots) & keep
        logits = 64.0 * (dot3(unit, rows, NT) * scale - jnp.where(hot, 0.4, 0.0))
        exps = jnp.where(keep, jnp.exp(logits), 0.0)
        total = jnp.sum(exps, axis=1, keepdims=True)
        at_label = jnp.sum(jnp.where(hot, logits, 0.0), axis=1, keepdims=True)
        pulls = jnp.concatenate([exps * scale, jnp.where(hot, scale, 0.0)], axis=0)
        return total, at_label, dot3(pulls, rows)

    total = jnp.zeros((8, 1), F32)
    at_label = jnp.zeros((8, 1), F32)
    pulled = jnp.zeros((16, E), F32)
    for k in range(4):
        rows = qb[k * 512 : (k + 1) * 512, :]
        slots = lax.broadcasted_iota(jnp.int32, (8, 512), 1) + k * 512
        fresh = ((slots - shift + QUEUE) & (QUEUE - 1)) < GEN
        t, a, u = score(rows, slots, jnp.logical_not(fresh))
        total, at_label, pulled = total + t, at_label + a, pulled + u

    my_rows = pl.ds(pl.multiple_of(core * 32, 32), 32)

    other_rows = pl.ds(pl.multiple_of((1 - core) * 32, 32), 32)

    def pass_on(which):
        dst = pan.at[which, my_rows]
        remote(half.at[which], dst, sem.at[7], sem.at[8], peer(dc=1)).start()

    pass_on(rep)
    for k, (lo, dy) in enumerate(rep_moves):
        which = ((z_lo + lo) % 2) * 4 + (y_me - dy) % 4
        wait_bytes(half.at[which], rep_sem.at[k])
        pass_on(which)
    pan[:, my_rows, :] = half[...]
    wait_bytes(pan.at[:, other_rows], sem.at[8])

    rows = pan[...].reshape(GEN, E)
    j = lax.broadcasted_iota(jnp.int32, (8, GEN), 1)
    t, a, u = score(rows, (j + shift) & (QUEUE - 1), j >= 0)
    total, at_label, pulled = total + t, at_label + a, pulled + u
    loss = jnp.log(total) - at_label
    lanes = lax.broadcasted_iota(jnp.int32, (8, 128), 1)
    rows128 = lax.broadcasted_iota(jnp.int32, (8, 128), 0)
    loss_out[...] = jnp.sum(jnp.where(lanes == rows128, loss, 0.0), axis=0)[:IMG]
    d_unit = 64.0 * (pulled[0:8] / total - pulled[8:16])
    d_embed = (d_unit - unit * jnp.sum(d_unit * unit, axis=1, keepdims=True)) * inv_len
    d_embed = jnp.where(rows8 < IMG, d_embed, 0.0)
    d_pooled = dot3(d_embed, head[...], NT)

    for b in range(IMG):
        for s in range(3):
            sd[b, 16:240, s * C : (s + 1) * C] = (
                spm[s] * d_pooled[b : b + 1, :]
            ).astype(BF16)

    po_h = po.astype(BF16).astype(F32)
    de_h = d_embed.astype(BF16).astype(F32)
    left = jnp.concatenate([po_h, po_h, po - po_h, jnp.zeros_like(po)], axis=0)
    right = jnp.concatenate(
        [de_h, d_embed - de_h, de_h, jnp.zeros_like(d_embed)], axis=0
    )
    g_head = dot(left.T.astype(BF16), right.astype(BF16))
    zsf2 = hgf
    for k in range(2):
        for h in range(2):
            zsf2[pl.ds(k * 512 + h, 256, stride=2), :] = g_head[
                :, h * 256 + k * 128 : h * 256 + (k + 1) * 128
            ]
    for k in range(2):
        gb.reshape(ROWS, C)[2 * CONV_ROWS :, k * 128 : (k + 1) * 128] = zsf2[
            k * 512 : (k + 1) * 512, :
        ].astype(BF16)

    flat = gb.reshape(ROWS, C)

    def weight_grad(turned, buf, tap, base):
        r, s = 2 - tap // 3, 2 - tap % 3
        rows = buf[:, r * 16 : r * 16 + 256, s * C : (s + 1) * C].reshape(IMG * 256, C)
        flat[base + tap * 256 : base + (tap + 1) * 256, :] = dot(turned[...], rows).astype(
            BF16
        )

    def send(u, first, count):
        at = pl.ds(4 * u + first, count)
        src, dst = gb.at[at, 1 - core], r1.at[at]
        remote(src, dst, sem.at[9], core_sem.at[u], peer(dc=1)).start()

    def two(*taps):
        for tap in taps:
            weight_grad(ht, sd, tap, CONV_ROWS)

    def one(*taps):
        for tap in taps:
            weight_grad(xt, sp, tap, 0)

    def back(i, _):
        b = 2 * i
        out = conv(sd, w2t, b) * fac[pl.ds(b, 2)].reshape(2 * CELLS, C)
        shifted(sp, b, out)
        return 0

    def after_core(u):
        wait_bytes(r1.at[pl.ds(4 * u, 4)], core_sem.at[u])
        for x in range(4):
            a = 4 * u + x
            v = gb[a, core].astype(F32) + r1[a].astype(F32)
            ta[a] = v[:, 0:128].astype(BF16)
            for lo in range(2):
                for y in range(4):
                    k, at = (lo * 4 + y) * CHUNK, (x * 2 + lo) * CHUNK
                    tbf[y, at : at + CHUNK, :] = v[k : k + CHUNK, 128:256]
        tb[u] = tbf[...].astype(BF16)
        for k in (1, 3, 2):
            src = ta.at[4 * u + (x_me + k) % 4]
            remote(src, ra.at[u, k - 1], sem.at[10], first_sem.at[u], peer(dx=k)).start()
            src = tb.at[u, (y_me + k) % 4]
            remote(src, ra.at[u, k + 2], sem.at[10], first_sem.at[u], peer(dy=k)).start()

    def after_first(u):
        wait_bytes(ra.at[u], first_sem.at[u])
        v = ta[4 * u + x_me].astype(F32)
        for k in range(3):
            v += ra[u, k].astype(F32)
        for lo in range(2):
            for y in range(4):
                k, at = (lo * 4 + y) * CHUNK, lo * CHUNK
                uaf[y, at : at + CHUNK, :] = v[k : k + CHUNK]
        v = tb[u, y_me].astype(F32)
        for k in range(3):
            v += ra[u, k + 3].astype(F32)
        for x in range(4):
            ubf[x, 0:40, :] = v[x * 40 : (x + 1) * 40]
        ua[u] = uaf[...].astype(BF16)
        ub[u] = ubf[...].astype(BF16)
        for k in (1, 3, 2):
            src = ua.at[u, (y_me + k) % 4]
            remote(src, ra2.at[u, k - 1], sem.at[11], second_sem.at[u], peer(dy=k)).start()
            src = ub.at[u, (x_me + k) % 4]
            remote(src, ra2.at[u, k + 2], sem.at[11], second_sem.at[u], peer(dx=k)).start()

    def after_second(u):
        wait_bytes(ra2.at[u], second_sem.at[u])
        for side, own in enumerate((ua[u, y_me], ub[u, x_me])):
            v = own.astype(F32)
            for k in range(3):
                v += ra2[u, 3 * side + k].astype(F32)
            for lo in range(2):
                zsf[2 * u + lo, side * CHUNK : (side + 1) * CHUNK, :] = v[
                    lo * CHUNK : (lo + 1) * CHUNK
                ]

    def renew(k, _):
        at = pl.ds(pl.multiple_of(k * 256, 256), 256)
        slot = lax.broadcasted_iota(jnp.int32, (256, GEN), 0) + k * 256
        source = (slot - shift + QUEUE) & (QUEUE - 1)
        pick = jnp.where(
            source == lax.broadcasted_iota(jnp.int32, (256, GEN), 1), 1.0, 0.0
        ).astype(BF16)
        new = dot(pick, pan[...].reshape(GEN, E))
        old = qb[at, :].astype(F32)
        fresh_out[at, :] = jnp.where(source[:, 0:1] < GEN, new, old).astype(BF16)
        return 0

    two(6, 7, 8)
    send(3, 0, 4)
    two(1, 2, 3, 4, 5)
    send(2, 0, 4)
    two(0)
    lax.fori_loop(0, 1, back, 0)
    after_core(3)
    lax.fori_loop(1, IMG // 2, back, 0)
    after_core(2)
    one(5, 6, 7, 8)
    send(1, 0, 4)
    one(0, 1, 2)
    send(0, 0, 2)
    one(3, 4)
    send(0, 2, 2)
    after_core(1)
    after_core(0)
    after_first(3)
    after_first(2)
    lax.fori_loop(0, 4, renew, 0)
    after_first(1)
    after_first(0)
    lax.fori_loop(4, 8, renew, 0)
    after_second(3)
    after_second(2)
    after_second(1)
    after_second(0)

    for z in range(8):
        zs[z] = zsf[z].astype(BF16)
    for k in (1, 7, 2, 6, 3, 5, 4):
        src = zs.at[(z_me + k) % 8]
        remote(src, zr.at[k - 1], sem.at[12], sem.at[13], peer(dz=k)).start()
    wait_bytes(zr, sem.at[13])
    v = zsf[z_me]
    for k in range(7):
        v += zr[k].astype(F32)
    low, high = v[0:CHUNK], v[CHUNK : 2 * CHUNK]

    row = first_row + lax.broadcasted_iota(jnp.int32, (CHUNK, 128), 0)
    in_one = row < CONV_ROWS
    in_head = row >= 2 * CONV_ROWS
    in_two = jnp.logical_not(in_one | in_head)
    sq = low * low + high * high
    for k, m in enumerate((in_one, in_two, in_head)):
        ns[0, k : k + 1, :] = jnp.sum(jnp.where(m, sq, 0.0), axis=0, keepdims=True)
    ns[0, 3:8, :] = jnp.zeros((5, 128), F32)

    def gather_sums(level, dst, moves):
        there, here = sem.at[14 + 2 * level], sem.at[15 + 2 * level]
        for k, m in enumerate(moves):
            remote(ns.at[level], dst.at[k], there, here, peer(**m)).start()
        wait_bytes(dst, here)
        s = ns[level]
        for k in range(len(moves)):
            s += dst[k]
        return s

    ns[1] = gather_sums(0, nr1, [dict(dx=a, dy=b) for a, b in XY])
    ns[2] = gather_sums(1, nr2, [dict(dz=k) for k in range(1, 8)])
    s = gather_sums(2, nr3, [dict(dc=1)])
    s = jnp.sum(s, axis=1, keepdims=True)
    scale = lax.rsqrt(s + 1e-06)
    conv_n, head_n = (9 * C * C) ** 0.5, (C * E) ** 0.5
    factor = jnp.where(
        in_one,
        scale[0:1] * conv_n,
        jnp.where(in_two, scale[1:2] * conv_n, scale[2:3] * head_n),
    )
    upd_out[pl.ds(0, CHUNK, stride=2), :] = low * factor
    upd_out[pl.ds(1, CHUNK, stride=2), :] = high * factor

    p_core.wait_send()
    sent = [
        (x_rec, 2),
        (z_rec, 4),
        (half.at[pl.ds(0, 7)], 6),
        (half, 7),
        (r1, 9),
        (ra, 10),
        (ra2, 11),
        (zr, 12),
        (nr1, 14),
        (nr2, 16),
        (nr3, 18),
    ]
    for ref, k in sent:
        wait_bytes(ref, sem.at[k])


SCRATCH = [
    pltpu.SMEM((IMG,), jnp.int32),
    pltpu.SMEM((32,), jnp.int32),
    pltpu.SMEM((1,), jnp.int32),
    VMEM((1, C), F32),
    VMEM((SIDE * SIDE, C), F32),
    VMEM((C, E), BF16),
    VMEM((64, E), BF16),
    VMEM((IMG, SIDE, SIDE, C), BF16),
    VMEM((3, 3, C, C), BF16),
    VMEM((3, 3, C, C), BF16),
    VMEM((3, 3, C, C), BF16),
    VMEM((QUEUE, E), BF16),
    VMEM((IMG, TALL, 3 * C), BF16),
    VMEM((IMG, TALL, 3 * C), BF16),
    VMEM((IMG, TALL, 3 * C), BF16),
    VMEM((IMG, TALL, 3 * C), BF16),
    VMEM((C, IMG * 256), BF16),
    VMEM((C, IMG * 256), BF16),
    VMEM((IMG, CELLS, C), F32),
    VMEM((3, CELLS, C), F32),
    VMEM((8, C), F32),
    VMEM((64, E), BF16),
    VMEM((32, E), BF16),
    VMEM((32, E), BF16),
    VMEM((3, 32, E), BF16),
    VMEM((32, E), BF16),
    VMEM((3, 32, E), BF16),
    VMEM((8, 32, E), BF16),
    VMEM((8, 64, E), BF16),
    VMEM((16, 2, 160, C), BF16),
    VMEM((16, 160, C), BF16),
    VMEM((16, 160, 128), BF16),
    VMEM((4, 160, 128), F32),
    VMEM((4, 4, 160, 128), BF16),
    VMEM((4, 6, 160, 128), BF16),
    VMEM((4, 48, 128), F32),
    VMEM((4, 4, 48, 128), BF16),
    VMEM((4, 48, 128), F32),
    VMEM((4, 4, 48, 128), BF16),
    VMEM((4, 6, 48, 128), BF16),
    VMEM((8, 48, 128), F32),
    VMEM((8, 48, 128), BF16),
    VMEM((7, 48, 128), BF16),
    VMEM((3, 8, 128), F32),
    VMEM((15, 8, 128), F32),
    VMEM((7, 8, 128), F32),
    VMEM((1, 8, 128), F32),
    VMEM((1024, 128), F32),
    DMA((11,)),
    DMA((20,)),
    DMA((7,)),
    DMA((4,)),
    DMA((4,)),
    DMA((4,)),
]


def shards(
    images,
    labels,
    conv_one,
    conv_two,
    prelu_slope,
    spatial,
    head_weight,
    class_queue,
    candidates,
    generator,
    offset,
):
    far = pl.BlockSpec(memory_space=pl.ANY)
    near = pl.BlockSpec(memory_space=pltpu.VMEM)
    loss, fresh, update = pl.pallas_call(
        kernel,
        out_shape=(
            VMEM((IMG,), F32),
            VMEM((QUEUE, E), BF16),
            VMEM((2 * CHUNK, 128), F32),
        ),
        in_specs=[far] * 11,
        out_specs=(near, near, near),
        scratch_shapes=SCRATCH,
        name="whole_step",
        compiler_params=pltpu.CompilerParams(
            collective_id=0, has_side_effects=True, vmem_limit_bytes=56 << 20
        ),
    )(
        images,
        labels,
        conv_one,
        conv_two,
        prelu_slope.reshape(1, C),
        spatial,
        head_weight,
        class_queue,
        candidates,
        generator,
        offset,
    )
    return loss, fresh, update.reshape(2 * CHUNK * 128)


def solution(mesh):
    in_specs = (
        P(("dp", "rep"), None, None, None),
        P(("dp", "rep")),
        P(),
        P(),
        P(),
        P(),
        P(),
        P(),
        P(("dp", "rep"), None),
        P(),
        P(),
    )
    out_specs = (P(("dp", "rep")), P(), P(("dp", "rep")))
    return jax.shard_map(
        shards, mesh=mesh, in_specs=in_specs, out_specs=out_specs, check_vma=False
    )
```

time: 79.2 us -> 68.4 us (0.86)
  Pallas kernels: 72.9 us -> 64.6 us
  local copies, waits for them, and re-layouts: 4.84 us -> 2.44 us
    pallas_call x1, Pallas kernels: 72.9 us -> 64.6 us  [shards(): pl.pallas_call(kernel, out_shape=(VMEM((IMG,), F32), VMEM((QUEUE, E), BF1...]
    unnamed x4 -> x3, local copies, waits for them, and re-layouts: 3.67 us -> 2.44 us
    squeeze x1 -> x0, local copies, waits for them, and re-layouts: 1.17 us -> none  [shards(): return (loss[0, :IMG], fresh, update.reshape(2 * CHUNK * 128))]
where the time goes in v2:
time: 68.4 us
  Pallas kernels  64.6 us (94%)
  local copies, waits for them, and re-layouts  2.44 us (4%)
  between operations  1.29 us (2%)
    pallas_call x1, Pallas kernels, shards(): pl.pallas_call(kernel, out_shape=(VMEM((IMG,), F32), VMEM((QUEUE, E), BF1...  64.6 us
    unnamed x3, local copies, waits for them, and re-layouts  2.44 us

profile of v2, /device:TPU:1, one launch (start us, length us, event | category | flops | bytes accessed | tf_op | source)
XLA Modules:
  0.0 68.4 jit_solution(11606067309765168589)
XLA Ops:
  1.3 64.6 %whole_step.1 = (f32[6]{0:T(128)S(1)}, bf16[2048,512]{1,0:T(8,128)(2,1)S(1)}, f32[40,128]{1,0:T(8,128)S(1)}) custom-call(bf16[6,14,14,256]{3,2,1,0:T(8,128)(2,1)} %img_hbm.1, s32[6]{0:T(128)} %lab_hbm.1, bf16[3,3,256,256]{3,2,1,0:T(8,128)(2,1)} %one_hbm.1, bf16[3,3,256,256]{3,2,1,0:T(8,128)(2,1)} %two_hbm.1, f32[1,256]{1,0:T(1,128)} %bitcast.3, ...), custom_call_target="tpu_custom_call" | custom-call | tf_op jit(solution)/shard_map/whole_step/pallas_call | solution.py:647
  65.9 0.5 copy.17
  66.4 0.6 copy.19
  67.0 1.3 %copy.18 = bf16[2048,512]{1,0:T(8,128)(2,1)} copy(bf16[2048,512]{1,0:T(8,128)(2,1)S(1)} %get-tuple-element.10) | data formatting | bytes 4194304

commit v3 on v2

--- a/solution.py
+++ b/solution.py
@@ -67,7 +67,11 @@
     return lax.rsqrt(total[:8] + 1e-06)
 
 
+HOPS = (0, 1, 2, 1)
 XY = [(dx, dy) for dx in range(4) for dy in range(4) if dx or dy]
+XY.sort(key=lambda m: -HOPS[m[0]] - HOPS[m[1]])
+RING4 = (2, 1, 3)
+RING8 = (4, 3, 5, 2, 6, 1, 7)
 
 
 def kernel(
@@ -175,13 +179,13 @@
         name: pltpu.make_async_copy(a, b, ld_sem.at[k])
         for k, (name, (a, b)) in enumerate(pairs.items())
     }
-    for cp in loads.values():
-        cp.start()
+    loads["cand"].start()
+    loads["gen"].start()
 
     barrier = pltpu.get_barrier_semaphore()
-    friends = [dict(dc=1)] + [dict(dx=a, dy=b) for a, b in XY]
-    friends += [dict(dz=k) for k in range(1, 8)]
-    friends += [dict(dlo=1, dy=k) for k in range(1, 4)]
+    friends = [dict(dx=a, dy=b) for a, b in XY]
+    friends += [dict(dz=k) for k in RING8]
+    friends += [dict(dlo=1, dy=k) for k in RING4] + [dict(dc=1)]
     for f in friends:
         pl.semaphore_signal(barrier, inc=1, device_id=peer(**f), device_id_type=MESH)
 
@@ -195,6 +199,9 @@
     p_core = remote(other_half, c_rec, sem.at[0], sem.at[1], peer(dc=1))
     p_core.start()
 
+    for name, cp in loads.items():
+        if name not in ("cand", "gen"):
+            cp.start()
     for buf in (s1, s2, sd, sp):
         for b in range(IMG):
             buf[b, 0:16, :] = jnp.zeros((16, 3 * C), BF16)
@@ -238,7 +245,7 @@
     p_core.wait_recv()
     own_half = cm[pl.ds(pl.multiple_of(core * 32, 32), 32)]
     ch[...] = (own_half.astype(F32) + c_rec[...].astype(F32)).astype(BF16)
-    for k in (1, 3, 2):
+    for k in RING4:
         remote(ch, x_rec.at[k - 1], sem.at[2], sem.at[3], peer(dx=k)).start()
 
     loads["w1"].wait()
@@ -269,7 +276,7 @@
     for k in range(3):
         whole += x_rec[k].astype(F32)
     ch2[...] = whole.astype(BF16)
-    for k in (1, 3, 2):
+    for k in RING4:
         remote(ch2, z_rec.at[k - 1], sem.at[4], sem.at[5], peer(dz=2 * k)).start()
 
     loads["spatial"].wait()
@@ -294,7 +301,7 @@
     for k in range(3):
         whole += z_rec[k].astype(F32)
     half[rep] = whole.astype(BF16)
-    rep_moves = [(lo, dy) for lo in range(2) for dy in range(4) if lo or dy]
+    rep_moves = [(1, 2), (1, 1), (1, 3), (0, 2), (0, 1), (0, 3), (1, 0)]
     for k, (lo, dy) in enumerate(rep_moves):
         to = peer(dlo=lo, dy=dy)
         remote(half.at[rep], half.at[rep], sem.at[6], rep_sem.at[k], to).start()
@@ -347,16 +354,21 @@
         remote(half.at[which], dst, sem.at[7], sem.at[8], peer(dc=1)).start()
 
     pass_on(rep)
-    for k, (lo, dy) in enumerate(rep_moves):
+    for k in range(6, -1, -1):
+        lo, dy = rep_moves[k]
         which = ((z_lo + lo) % 2) * 4 + (y_me - dy) % 4
         wait_bytes(half.at[which], rep_sem.at[k])
         pass_on(which)
+
+    j = lax.broadcasted_iota(jnp.int32, (8, GEN // 2), 1)
+    j = (j >> 5) * 64 + (j & 31) + shift
+    rows = half[...].reshape(GEN // 2, E)
+    t, a, u = score(rows, (j + core * 32) & (QUEUE - 1), j >= 0)
+    total, at_label, pulled = total + t, at_label + a, pulled + u
     pan[:, my_rows, :] = half[...]
     wait_bytes(pan.at[:, other_rows], sem.at[8])
-
-    rows = pan[...].reshape(GEN, E)
-    j = lax.broadcasted_iota(jnp.int32, (8, GEN), 1)
-    t, a, u = score(rows, (j + shift) & (QUEUE - 1), j >= 0)
+    rows = pan[:, other_rows, :].reshape(GEN // 2, E)
+    t, a, u = score(rows, (j + (1 - core) * 32) & (QUEUE - 1), j >= 0)
     total, at_label, pulled = total + t, at_label + a, pulled + u
     loss = jnp.log(total) - at_label
     lanes = lax.broadcasted_iota(jnp.int32, (8, 128), 1)
@@ -419,55 +431,71 @@
         shifted(sp, b, out)
         return 0
 
-    def after_core(u):
-        wait_bytes(r1.at[pl.ds(4 * u, 4)], core_sem.at[u])
-        for x in range(4):
-            a = 4 * u + x
-            v = gb[a, core].astype(F32) + r1[a].astype(F32)
-            ta[a] = v[:, 0:128].astype(BF16)
+    def after_core(u, n):
+        for unit in range(u, u + n):
+            wait_bytes(r1.at[pl.ds(4 * unit, 4)], core_sem.at[unit])
+            for x in range(4):
+                a = 4 * unit + x
+                v = gb[a, core].astype(F32) + r1[a].astype(F32)
+                ta[unit, x] = v[:, 0:128].astype(BF16)
+                for lo in range(2):
+                    for y in range(4):
+                        k, at = (lo * 4 + y) * CHUNK, (x * 2 + lo) * CHUNK
+                        tbf[y, at : at + CHUNK, :] = v[k : k + CHUNK, 128:256]
+            tb[unit] = tbf[...].astype(BF16)
+        span, there, here = pl.ds(u, n), sem.at[10], first_sem.at[u]
+        for k in RING4:
+            src = ta.at[span, (x_me + k) % 4]
+            remote(src, ra.at[k - 1, span], there, here, peer(dx=k)).start()
+            src = tb.at[span, (y_me + k) % 4]
+            remote(src, ra.at[k + 2, span], there, here, peer(dy=k)).start()
+
+    def after_first(u, n):
+        wait_bytes(ra.at[:, pl.ds(u, n)], first_sem.at[u])
+        for unit in range(u, u + n):
+            v = ta[unit, x_me].astype(F32)
+            for k in range(3):
+                v += ra[k, unit].astype(F32)
             for lo in range(2):
                 for y in range(4):
-                    k, at = (lo * 4 + y) * CHUNK, (x * 2 + lo) * CHUNK
-                    tbf[y, at : at + CHUNK, :] = v[k : k + CHUNK, 128:256]
-        tb[u] = tbf[...].astype(BF16)
-        for k in (1, 3, 2):
-            src = ta.at[4 * u + (x_me + k) % 4]
-            remote(src, ra.at[u, k - 1], sem.at[10], first_sem.at[u], peer(dx=k)).start()
-            src = tb.at[u, (y_me + k) % 4]
-            remote(src, ra.at[u, k + 2], sem.at[10], first_sem.at[u], peer(dy=k)).start()
-
-    def after_first(u):
-        wait_bytes(ra.at[u], first_sem.at[u])
-        v = ta[4 * u + x_me].astype(F32)
-        for k in range(3):
-            v += ra[u, k].astype(F32)
-        for lo in range(2):
-            for y in range(4):
-                k, at = (lo * 4 + y) * CHUNK, lo * CHUNK
-                uaf[y, at : at + CHUNK, :] = v[k : k + CHUNK]
-        v = tb[u, y_me].astype(F32)
-        for k in range(3):
-            v += ra[u, k + 3].astype(F32)
-        for x in range(4):
-            ubf[x, 0:40, :] = v[x * 40 : (x + 1) * 40]
-        ua[u] = uaf[...].astype(BF16)
-        ub[u] = ubf[...].astype(BF16)
-        for k in (1, 3, 2):
-            src = ua.at[u, (y_me + k) % 4]
-            remote(src, ra2.at[u, k - 1], sem.at[11], second_sem.at[u], peer(dy=k)).start()
-            src = ub.at[u, (x_me + k) % 4]
-            remote(src, ra2.at[u, k + 2], sem.at[11], second_sem.at[u], peer(dx=k)).start()
-
-    def after_second(u):
-        wait_bytes(ra2.at[u], second_sem.at[u])
-        for side, own in enumerate((ua[u, y_me], ub[u, x_me])):
-            v = own.astype(F32)
+                    k, at = (lo * 4 + y) * CHUNK, lo * CHUNK
+                    uaf[y, at : at + CHUNK, :] = v[k : k + CHUNK]
+            v = tb[unit, y_me].astype(F32)
             for k in range(3):
-                v += ra2[u, 3 * side + k].astype(F32)
-            for lo in range(2):
-                zsf[2 * u + lo, side * CHUNK : (side + 1) * CHUNK, :] = v[
-                    lo * CHUNK : (lo + 1) * CHUNK
-                ]
+                v += ra[k + 3, unit].astype(F32)
+            for x in range(4):
+                ubf[x, 0:40, :] = v[x * 40 : (x + 1) * 40]
+            ua[unit] = uaf[...].astype(BF16)
+            ub[unit] = ubf[...].astype(BF16)
+        span, there, here = pl.ds(u, n), sem.at[11], second_sem.at[u]
+        for k in RING4:
+            src = ua.at[span, (y_me + k) % 4]
+            remote(src, ra2.at[k - 1, span], there, here, peer(dy=k)).start()
+            src = ub.at[span, (x_me + k) % 4]
+            remote(src, ra2.at[k + 2, span], there, here, peer(dx=k)).start()
+
+    def after_second(u, n):
+        wait_bytes(ra2.at[:, pl.ds(u, n)], second_sem.at[u])
+        for unit in range(u, u + n):
+            for side, own in enumerate((ua[unit, y_me], ub[unit, x_me])):
+                v = own.astype(F32)
+                for k in range(3):
+                    v += ra2[3 * side + k, unit].astype(F32)
+                for lo in range(2):
+                    zsf[2 * unit + lo, side * CHUNK : (side + 1) * CHUNK, :] = v[
+                        lo * CHUNK : (lo + 1) * CHUNK
+                    ]
+
+    def send_z(upper):
+        for z in range(4 * upper, 4 * upper + 4):
+            zs[z] = zsf[z].astype(BF16)
+        for k in RING8:
+            to = (z_me + k) % 8
+
+            @pl.when(to // 4 == upper)
+            def _():
+                dst = zr.at[k - 1]
+                remote(zs.at[to], dst, sem.at[12], sem.at[13], peer(dz=k)).start()
 
     def renew(k, _):
         at = pl.ds(pl.multiple_of(k * 256, 256), 256)
@@ -486,34 +514,27 @@
     two(1, 2, 3, 4, 5)
     send(2, 0, 4)
     two(0)
-    lax.fori_loop(0, 1, back, 0)
-    after_core(3)
-    lax.fori_loop(1, IMG // 2, back, 0)
-    after_core(2)
+    lax.fori_loop(0, 2, back, 0)
+    after_core(2, 2)
+    lax.fori_loop(2, IMG // 2, back, 0)
     one(5, 6, 7, 8)
     send(1, 0, 4)
     one(0, 1, 2)
     send(0, 0, 2)
     one(3, 4)
     send(0, 2, 2)
-    after_core(1)
-    after_core(0)
-    after_first(3)
-    after_first(2)
+    after_core(1, 1)
+    after_core(0, 1)
+    after_first(2, 2)
     lax.fori_loop(0, 4, renew, 0)
-    after_first(1)
-    after_first(0)
+    after_first(1, 1)
+    after_second(2, 2)
+    send_z(1)
+    after_first(0, 1)
     lax.fori_loop(4, 8, renew, 0)
-    after_second(3)
-    after_second(2)
-    after_second(1)
-    after_second(0)
-
-    for z in range(8):
-        zs[z] = zsf[z].astype(BF16)
-    for k in (1, 7, 2, 6, 3, 5, 4):
-        src = zs.at[(z_me + k) % 8]
-        remote(src, zr.at[k - 1], sem.at[12], sem.at[13], peer(dz=k)).start()
+    after_second(1, 1)
+    after_second(0, 1)
+    send_z(0)
     wait_bytes(zr, sem.at[13])
     v = zsf[z_me]
     for k in range(7):
@@ -540,7 +561,7 @@
         return s
 
     ns[1] = gather_sums(0, nr1, [dict(dx=a, dy=b) for a, b in XY])
-    ns[2] = gather_sums(1, nr2, [dict(dz=k) for k in range(1, 8)])
+    ns[2] = gather_sums(1, nr2, [dict(dz=k) for k in RING8])
     s = gather_sums(2, nr3, [dict(dc=1)])
     s = jnp.sum(s, axis=1, keepdims=True)
     scale = lax.rsqrt(s + 1e-06)
@@ -603,15 +624,15 @@
     VMEM((8, 64, E), BF16),
     VMEM((16, 2, 160, C), BF16),
     VMEM((16, 160, C), BF16),
-    VMEM((16, 160, 128), BF16),
+    VMEM((4, 4, 160, 128), BF16),
     VMEM((4, 160, 128), F32),
     VMEM((4, 4, 160, 128), BF16),
-    VMEM((4, 6, 160, 128), BF16),
+    VMEM((6, 4, 160, 128), BF16),
     VMEM((4, 48, 128), F32),
     VMEM((4, 4, 48, 128), BF16),
     VMEM((4, 48, 128), F32),
     VMEM((4, 4, 48, 128), BF16),
-    VMEM((4, 6, 48, 128), BF16),
+    VMEM((6, 4, 48, 128), BF16),
     VMEM((8, 48, 128), F32),
     VMEM((8, 48, 128), BF16),
     VMEM((7, 48, 128), BF16),

time: 68.4 us -> 66.4 us (0.971)
  Pallas kernels: 64.6 us -> 62.5 us
    pallas_call x1, Pallas kernels: 64.6 us -> 62.5 us  [shards(): pl.pallas_call(kernel, out_shape=(VMEM((IMG,), F32), VMEM((QUEUE, E), BF1...]
where the time goes in v3:
time: 66.4 us; the launch traced here: 66.2 us
  Pallas kernels  62.5 us (94%)
  local copies, waits for them, and re-layouts  2.44 us (4%)
  between operations  1.29 us (2%)
    pallas_call x1, Pallas kernels, shards(): pl.pallas_call(kernel, out_shape=(VMEM((IMG,), F32), VMEM((QUEUE, E), BF1...  62.5 us
    unnamed x3, local copies, waits for them, and re-layouts  2.44 us

profile of v3, /device:TPU:1, one launch (start us, length us, event | category | flops | bytes accessed | tf_op | source)
XLA Modules:
  0.0 66.2 jit_solution(9348210678904604119)
XLA Ops:
  1.3 62.5 %whole_step.1 = (f32[6]{0:T(128)S(1)}, bf16[2048,512]{1,0:T(8,128)(2,1)S(1)}, f32[40,128]{1,0:T(8,128)S(1)}) custom-call(bf16[6,14,14,256]{3,2,1,0:T(8,128)(2,1)} %img_hbm.1, s32[6]{0:T(128)} %lab_hbm.1, bf16[3,3,256,256]{3,2,1,0:T(8,128)(2,1)} %one_hbm.1, bf16[3,3,256,256]{3,2,1,0:T(8,128)(2,1)} %two_hbm.1, f32[1,256]{1,0:T(1,128)} %bitcast.3, ...), custom_call_target="tpu_custom_call" | custom-call | tf_op jit(solution)/shard_map/whole_step/pallas_call | solution.py:668
  63.8 0.5 copy.17
  64.3 0.6 copy.19
  64.9 1.3 %copy.18 = bf16[2048,512]{1,0:T(8,128)(2,1)} copy(bf16[2048,512]{1,0:T(8,128)(2,1)S(1)} %get-tuple-element.10) | data formatting | bytes 4194304

commit v4 on v3

--- a/solution.py
+++ b/solution.py
@@ -109,6 +109,8 @@
     ht,
     fac,
     spm,
+    spb,
+    g2,
     pooled,
     cm,
     c_rec,
@@ -227,7 +229,10 @@
             part = v[k * CELLS : (k + 1) * CELLS]
             tall = jnp.concatenate([part, jnp.zeros((32, C), F32)], axis=0)
             at = pl.ds(pl.multiple_of((b + k) * 256, 256), 256)
-            buf[:, at] = tall.T.astype(BF16)
+            if buf is ht:
+                buf[at, :] = tall.T.astype(BF16)
+            else:
+                buf[:, at] = tall.T.astype(BF16)
 
     loads["img"].wait()
 
@@ -283,6 +288,19 @@
     for p in range(SIDE):
         spm[1, p * PAD : p * PAD + SIDE, :] = spatial[p * SIDE : (p + 1) * SIDE, :]
         spm[1, p * PAD + SIDE : (p + 1) * PAD, :] = jnp.zeros((PAD - SIDE, C), F32)
+    spm[0] = pltpu.roll(spm[1], 1, 0)
+    spm[2] = pltpu.roll(spm[1], CELLS - 1, 0)
+    spb[0:16, :] = jnp.zeros((16, 3 * C), BF16)
+    spb[240:TALL, :] = jnp.zeros((TALL - 240, 3 * C), BF16)
+    for k in range(3):
+        spb[16:240, k * C : (k + 1) * C] = spm[k].astype(BF16)
+
+    def unscaled(*taps):
+        for tap in taps:
+            r, c = 2 - tap // 3, 2 - tap % 3
+            cells = spb[r * 16 : r * 16 + 256, c * C : (c + 1) * C]
+            g2[tap] = dot(ht[...], cells).reshape(IMG, C, C)
+
     loads["w2"].wait()
 
     def second(i, _):
@@ -295,6 +313,7 @@
         return 0
 
     lax.fori_loop(0, IMG // 2, second, 0)
+    unscaled(0, 1, 2, 3)
 
     wait_bytes(z_rec, sem.at[5])
     whole = ch2[...].astype(F32)
@@ -306,8 +325,6 @@
         to = peer(dlo=lo, dy=dy)
         remote(half.at[rep], half.at[rep], sem.at[6], rep_sem.at[k], to).start()
 
-    spm[0] = pltpu.roll(spm[1], 1, 0)
-    spm[2] = pltpu.roll(spm[1], CELLS - 1, 0)
     for r in range(3):
         for s in range(3):
             turned = w2[2 - r, 2 - s].astype(F32).T
@@ -315,6 +332,7 @@
 
     for name in ("head", "lab", "off", "queue"):
         loads[name].wait()
+    unscaled(4, 5, 6, 7, 8)
     po = pooled[...]
     embed = dot3(po, head[...])
     inv_len = lax.rsqrt(jnp.sum(embed * embed, axis=1, keepdims=True) + 1e-06)
@@ -379,12 +397,6 @@
     d_embed = jnp.where(rows8 < IMG, d_embed, 0.0)
     d_pooled = dot3(d_embed, head[...], NT)
 
-    for b in range(IMG):
-        for s in range(3):
-            sd[b, 16:240, s * C : (s + 1) * C] = (
-                spm[s] * d_pooled[b : b + 1, :]
-            ).astype(BF16)
-
     po_h = po.astype(BF16).astype(F32)
     de_h = d_embed.astype(BF16).astype(F32)
     left = jnp.concatenate([po_h, po_h, po - po_h, jnp.zeros_like(po)], axis=0)
@@ -419,7 +431,11 @@
 
     def two(*taps):
         for tap in taps:
-            weight_grad(ht, sd, tap, CONV_ROWS)
+            v = g2[tap, 0] * d_pooled[0:1, :]
+            for b in range(1, IMG):
+                v += g2[tap, b] * d_pooled[b : b + 1, :]
+            at = CONV_ROWS + tap * 256
+            flat[at : at + 256, :] = v.astype(BF16)
 
     def one(*taps):
         for tap in taps:
@@ -514,6 +530,11 @@
     two(1, 2, 3, 4, 5)
     send(2, 0, 4)
     two(0)
+    for b in range(IMG):
+        for s in range(3):
+            sd[b, 16:240, s * C : (s + 1) * C] = (
+                spm[s] * d_pooled[b : b + 1, :]
+            ).astype(BF16)
     lax.fori_loop(0, 2, back, 0)
     after_core(2, 2)
     lax.fori_loop(2, IMG // 2, back, 0)
@@ -521,20 +542,20 @@
     send(1, 0, 4)
     one(0, 1, 2)
     send(0, 0, 2)
-    one(3, 4)
+    one(3)
+    after_core(1, 1)
+    one(4)
     send(0, 2, 2)
-    after_core(1, 1)
     after_core(0, 1)
     after_first(2, 2)
-    lax.fori_loop(0, 4, renew, 0)
     after_first(1, 1)
     after_second(2, 2)
     send_z(1)
     after_first(0, 1)
-    lax.fori_loop(4, 8, renew, 0)
     after_second(1, 1)
     after_second(0, 1)
     send_z(0)
+    lax.fori_loop(0, 8, renew, 0)
     wait_bytes(zr, sem.at[13])
     v = zsf[z_me]
     for k in range(7):
@@ -610,9 +631,11 @@
     VMEM((IMG, TALL, 3 * C), BF16),
     VMEM((IMG, TALL, 3 * C), BF16),
     VMEM((C, IMG * 256), BF16),
-    VMEM((C, IMG * 256), BF16),
+    VMEM((IMG * 256, 256), BF16),
     VMEM((IMG, CELLS, C), F32),
     VMEM((3, CELLS, C), F32),
+    VMEM((TALL, 3 * C), BF16),
+    VMEM((9, IMG, C, C), F32),
     VMEM((8, C), F32),
     VMEM((64, E), BF16),
     VMEM((32, E), BF16),

time: 66.4 us -> 66.2 us (level)
  no operation moved by 1% of the time
where the time goes in v4:
time: 66.2 us; the launch traced here: 66.1 us
  Pallas kernels  62.4 us (94%)
  local copies, waits for them, and re-layouts  2.44 us (4%)
  between operations  1.29 us (2%)
    pallas_call x1, Pallas kernels, shards(): pl.pallas_call(kernel, out_shape=(VMEM((IMG,), F32), VMEM((QUEUE, E), BF1...  62.4 us
    unnamed x3, local copies, waits for them, and re-layouts  2.44 us

profile of v4, /device:TPU:1, one launch (start us, length us, event | category | flops | bytes accessed | tf_op | source)
XLA Modules:
  0.0 66.1 jit_solution(17401660991775438860)
XLA Ops:
  1.3 62.4 %whole_step.1 = (f32[6]{0:T(128)S(1)}, bf16[2048,512]{1,0:T(8,128)(2,1)S(1)}, f32[40,128]{1,0:T(8,128)S(1)}) custom-call(bf16[6,14,14,256]{3,2,1,0:T(8,128)(2,1)} %img_hbm.1, s32[6]{0:T(128)} %lab_hbm.1, bf16[3,3,256,256]{3,2,1,0:T(8,128)(2,1)} %one_hbm.1, bf16[3,3,256,256]{3,2,1,0:T(8,128)(2,1)} %two_hbm.1, f32[1,256]{1,0:T(1,128)} %bitcast.3, ...), custom_call_target="tpu_custom_call" | custom-call | tf_op jit(solution)/shard_map/whole_step/pallas_call | solution.py:691
  63.6 0.5 copy.17
  64.2 0.6 copy.19
  64.8 1.3 %copy.18 = bf16[2048,512]{1,0:T(8,128)(2,1)} copy(bf16[2048,512]{1,0:T(8,128)(2,1)S(1)} %get-tuple-element.10) | data formatting | bytes 4194304

commit v5 on v3

--- a/solution.py
+++ b/solution.py
@@ -206,7 +206,7 @@
         for b in range(IMG):
             buf[b, 0:16, :] = jnp.zeros((16, 3 * C), BF16)
             buf[b, 240:TALL, :] = jnp.zeros((TALL - 240, 3 * C), BF16)
-    pooled[...] = jnp.zeros((8, C), F32)
+    pooled[...] = jnp.zeros((16, C), F32)
     uaf[...] = jnp.zeros((4, 48, 128), F32)
     ubf[...] = jnp.zeros((4, 48, 128), F32)
     zsf[...] = jnp.zeros((8, 48, 128), F32)
@@ -315,7 +315,7 @@
 
     for name in ("head", "lab", "off", "queue"):
         loads[name].wait()
-    po = pooled[...]
+    po = pooled[0:8, :]
     embed = dot3(po, head[...])
     inv_len = lax.rsqrt(jnp.sum(embed * embed, axis=1, keepdims=True) + 1e-06)
     unit = embed * inv_len
@@ -442,7 +442,7 @@
                     for y in range(4):
                         k, at = (lo * 4 + y) * CHUNK, (x * 2 + lo) * CHUNK
                         tbf[y, at : at + CHUNK, :] = v[k : k + CHUNK, 128:256]
-            tb[unit] = tbf[...].astype(BF16)
+            tb[unit] = tbf[:, 0:160, :].astype(BF16)
         span, there, here = pl.ds(u, n), sem.at[10], first_sem.at[u]
         for k in RING4:
             src = ta.at[span, (x_me + k) % 4]
@@ -571,8 +571,9 @@
         scale[0:1] * conv_n,
         jnp.where(in_two, scale[1:2] * conv_n, scale[2:3] * head_n),
     )
-    upd_out[pl.ds(0, CHUNK, stride=2), :] = low * factor
-    upd_out[pl.ds(1, CHUNK, stride=2), :] = high * factor
+    hgf[pl.ds(0, CHUNK, stride=2), :] = low * factor
+    hgf[pl.ds(1, CHUNK, stride=2), :] = high * factor
+    upd_out[...] = hgf[0 : 2 * CHUNK, :]
 
     p_core.wait_send()
     sent = [
@@ -613,7 +614,7 @@
     VMEM((C, IMG * 256), BF16),
     VMEM((IMG, CELLS, C), F32),
     VMEM((3, CELLS, C), F32),
-    VMEM((8, C), F32),
+    VMEM((16, C), F32),
     VMEM((64, E), BF16),
     VMEM((32, E), BF16),
     VMEM((32, E), BF16),
@@ -625,7 +626,7 @@
     VMEM((16, 2, 160, C), BF16),
     VMEM((16, 160, C), BF16),
     VMEM((4, 4, 160, 128), BF16),
-    VMEM((4, 160, 128), F32),
+    VMEM((4, 176, 128), F32),
     VMEM((4, 4, 160, 128), BF16),
     VMEM((6, 4, 160, 128), BF16),
     VMEM((4, 48, 128), F32),

time: 66.4 us -> 66.4 us (level)
  no operation moved by 1% of the time
where the time goes in v5:
time: 66.4 us; the launch traced here: 66.2 us
  Pallas kernels  62.5 us (94%)
  local copies, waits for them, and re-layouts  2.44 us (4%)
  between operations  1.29 us (2%)
    pallas_call x1, Pallas kernels, shards(): pl.pallas_call(kernel, out_shape=(VMEM((IMG,), F32), VMEM((QUEUE, E), BF1...  62.5 us
    unnamed x3, local copies, waits for them, and re-layouts  2.44 us

profile of v5, /device:TPU:1, one launch (start us, length us, event | category | flops | bytes accessed | tf_op | source)
XLA Modules:
  0.0 66.2 jit_solution(802909392478573977)
XLA Ops:
  1.3 62.5 %whole_step.1 = (f32[6]{0:T(128)S(1)}, bf16[2048,512]{1,0:T(8,128)(2,1)S(1)}, f32[40,128]{1,0:T(8,128)S(1)}) custom-call(bf16[6,14,14,256]{3,2,1,0:T(8,128)(2,1)} %img_hbm.1, s32[6]{0:T(128)} %lab_hbm.1, bf16[3,3,256,256]{3,2,1,0:T(8,128)(2,1)} %one_hbm.1, bf16[3,3,256,256]{3,2,1,0:T(8,128)(2,1)} %two_hbm.1, f32[1,256]{1,0:T(1,128)} %bitcast.3, ...), custom_call_target="tpu_custom_call" | custom-call | tf_op jit(solution)/shard_map/whole_step/pallas_call | solution.py:669
  63.8 0.5 copy.17
  64.3 0.6 copy.19
  64.9 1.3 %copy.18 = bf16[2048,512]{1,0:T(8,128)(2,1)} copy(bf16[2048,512]{1,0:T(8,128)(2,1)S(1)} %get-tuple-element.10) | data formatting | bytes 4194304
